TPU v7x, 512 devices: a whole 4x4x16 slice. The times are simulated.
512 devices in a mesh: emb: 128 (over y, z, core), col: 4 (over x).
Axes of the slice: x: 4, y: 4, z: 16, core: 2. Of those that a mesh axis runs over, the one named last changes fastest.
Arguments:
- user_table: bfloat16 [1024, 16384], P('emb', 'col'), may hold values from -4 to 4
- user_scale: bfloat16 [1024], P('emb'), may hold values from 0.5 to 2
- item_table: bfloat16 [4096, 1024], P('emb', 'col'), may hold values from -3 to 3
- user_owner: int32 [16384, 1], P('emb'), may hold values from 0 to 127; in each aligned block of 128 rows (0 to 127, 128 to 255, ...) at most 2 rows name the same one
- user_row: int32 [16384], P('emb'), may hold values from 0 to 7
- item_owner: int32 [16384, 4], P('emb'), may hold values from 0 to 127, all different within a row; in each aligned block of 128 rows (0 to 127, 128 to 255, ...) at most 8 rows name the same one
- item_row: int32 [16384, 4], P('emb'), may hold values from 0 to 31
- labels: float32 [16384], P('emb'), may hold values from 0 to 1
- enter_user: bfloat16 [16384, 128], P('col'), may hold values from -0.046875 to 0.046875
- enter_item: bfloat16 [1024, 128], P('col'), may hold values from -0.046875 to 0.046875
- leave_user: bfloat16 [128, 16384], P(None, 'col'), may hold values from -0.5 to 0.5
- leave_item: bfloat16 [128, 1024], P(None, 'col'), may hold values from -0.5 to 0.5
- bias_user: float32 [16384], P('col'), may hold values from -3 to 3
- bias_item: float32 [1024], P('col'), may hold values from -3 to 3
- head_user: float32 [16384], P('col'), may hold values from -0.046875 to 0.046875
- head_item: float32 [1024], P('col'), may hold values from -0.046875 to 0.046875
Outputs:
- user_grad: float32 [1024, 16384], P('emb', 'col')
- item_grad: float32 [4096, 1024], P('emb', 'col')
Inputs may be any that keep to these rules, and one draw needn't show every extreme that they name: `user_owner`: among the impressions of one device no owner is named more than 2 times; in some devices one owner is named exactly 2 times. `item_owner`: the 4 owners of one impression differ. Among the item entries of one device no owner is named more than 8 times; in some devices one owner exactly 8 times.
All inputs are finite; a program needn't handle non-finite values.
Results may differ from a plain program's by a relative error of at most 0.035.
Values may be sent and summed in bfloat16 or wider, within the bound.
No kernel may reach another device: no remote copies, remote signals or barrier semaphores. Data moves between devices by JAX's collectives and lax.ppermute only.
A program may use at most 64 MiB of HBM per device.

v0:
```python
import jax
import jax.numpy as jnp
from jax import lax
from jax.sharding import PartitionSpec as P

loss_scale = 128.0


def slot_index(owner_ids, owners, capacity):
    members = (owner_ids[:, None] == jnp.arange(owners, dtype=jnp.int32)[None, :]).astype(jnp.int32)
    earlier = jnp.cumsum(members, axis=0) - members
    rank_within = jnp.sum(earlier * members, axis=1)
    return owner_ids * capacity + rank_within


def contract(matrix, factor):
    return lax.dot_general(
        matrix, factor, (((1,), (1,)), ((), ())), preferred_element_type=jnp.float32
    )


def body(
    user_table,
    user_scale,
    item_table,
    user_owner,
    user_row,
    item_owner,
    item_row,
    labels,
    enter_user,
    enter_item,
    leave_user,
    leave_item,
    bias_user,
    bias_item,
    head_user,
    head_item,
):
    owners = lax.axis_size("emb")
    imp_rows = labels.shape[0]
    list_len = item_row.shape[1]
    user_cap = max(2, 3 * imp_rows // (2 * owners) + 1)
    item_cap = list_len * user_cap
    users_local = user_table.shape[0]
    items_local = item_table.shape[0]
    user_width = user_table.shape[1]
    item_width = item_table.shape[1]
    user_slot = slot_index(user_owner[:, 0], owners, user_cap)
    item_slot = slot_index(item_owner.reshape(-1), owners, item_cap)
    user_want = (
        jnp.zeros((owners * user_cap,), jnp.int32)
        .at[user_slot]
        .set(user_row)
        .reshape(owners, user_cap)
    )
    item_want = (
        jnp.zeros((owners * item_cap,), jnp.int32)
        .at[item_slot]
        .set(item_row.reshape(-1))
        .reshape(owners, user_cap, list_len)
    )
    user_ask = lax.all_to_all(user_want, "emb", split_axis=0, concat_axis=0, tiled=True)
    item_ask = lax.all_to_all(item_want, "emb", split_axis=0, concat_axis=0, tiled=True)
    found_rows = jnp.take(user_table, user_ask, axis=0)
    found_scale = jnp.take(user_scale, user_ask, axis=0)
    found_items = jnp.take(item_table, item_ask, axis=0)
    fetched = (
        lax.all_to_all(found_rows, "emb", split_axis=0, concat_axis=0, tiled=True),
        lax.all_to_all(found_scale, "emb", split_axis=0, concat_axis=0, tiled=True),
        lax.all_to_all(found_items, "emb", split_axis=0, concat_axis=0, tiled=True),
        user_ask,
        item_ask,
    )
    got_rows, got_scale, got_items, asked_users, asked_items = fetched
    item_input = jnp.take(
        got_items.reshape(owners * item_cap, item_width), item_slot, axis=0
    ).reshape(imp_rows, list_len, item_width)
    pooled = jnp.sum(item_input.astype(jnp.float32), axis=1).astype(jnp.bfloat16)
    item_float = pooled.astype(jnp.float32)
    item_scaled = (item_float * head_item).astype(jnp.bfloat16)
    item_low = jnp.dot(pooled, enter_item, preferred_element_type=jnp.float32)
    picked = jnp.take(got_rows.reshape(owners * user_cap, user_width), user_slot, axis=0)
    picked_scale = jnp.take(got_scale.reshape(-1), user_slot, axis=0)
    user_input = (picked.astype(jnp.float32) * picked_scale.astype(jnp.float32)[:, None]).astype(
        jnp.bfloat16
    )
    low_part = jnp.dot(user_input, enter_user, preferred_element_type=jnp.float32) + item_low
    lowrank = lax.psum(low_part.astype(jnp.bfloat16), "col")
    hidden_item = jnp.dot(lowrank, leave_item, preferred_element_type=jnp.float32)
    hidden_user = jnp.dot(lowrank, leave_user, preferred_element_type=jnp.float32)
    user_float = user_input.astype(jnp.float32)
    user_logit = jnp.sum(head_user * (user_float * (hidden_user + bias_user) + user_float), axis=1)
    user_scaled = (user_float * head_user).astype(jnp.bfloat16)
    user_carry = contract(user_scaled, leave_user)
    logit_part = user_logit + jnp.sum(
        head_item * (item_float * (hidden_item + bias_item) + item_float), axis=1
    )
    carry_part = user_carry + contract(item_scaled, leave_item)
    logits, carried = (
        lax.psum(logit_part.astype(jnp.bfloat16), "col").astype(jnp.float32),
        lax.psum(carry_part.astype(jnp.bfloat16), "col").astype(jnp.float32),
    )
    logit_grad = loss_scale * (jax.nn.sigmoid(logits) - labels)
    back_rank = (logit_grad[:, None] * carried).astype(jnp.bfloat16)
    item_delta = (
        logit_grad[:, None] * head_item * (hidden_item + bias_item + 1.0)
        + contract(back_rank, enter_item)
    ).astype(jnp.bfloat16)
    item_send = (
        jnp.zeros((owners * item_cap, item_width), jnp.bfloat16)
        .at[item_slot]
        .set(jnp.repeat(item_delta, list_len, axis=0))
        .reshape(owners, user_cap, list_len, item_width)
    )
    user_delta = (
        logit_grad[:, None] * head_user * (hidden_user + bias_user + 1.0)
        + contract(back_rank, enter_user)
    ).astype(jnp.bfloat16)
    user_send = (
        jnp.zeros((owners * user_cap, user_width), jnp.bfloat16)
        .at[user_slot]
        .set(user_delta)
        .reshape(owners, user_cap, user_width)
    )
    came_user, came_items = (
        lax.all_to_all(user_send, "emb", split_axis=0, concat_axis=0, tiled=True),
        lax.all_to_all(item_send, "emb", split_axis=0, concat_axis=0, tiled=True),
    )
    owner_rows = came_user.reshape(owners * user_cap, user_width)
    user_pick = (
        jnp.arange(users_local, dtype=jnp.int32)[:, None] == asked_users.reshape(-1)[None, :]
    ).astype(jnp.bfloat16)
    user_grad = jnp.dot(user_pick, owner_rows, preferred_element_type=jnp.float32)
    item_pick = (
        jnp.arange(items_local, dtype=jnp.int32)[:, None] == asked_items.reshape(-1)[None, :]
    ).astype(jnp.bfloat16)
    item_grad = jnp.dot(
        item_pick,
        came_items.reshape(owners * item_cap, item_width),
        preferred_element_type=jnp.float32,
    )
    return (user_grad, item_grad)


def solution(mesh):
    return jax.shard_map(
        body,
        mesh=mesh,
        in_specs=(
            P("emb", "col"),
            P("emb"),
            P("emb", "col"),
            P("emb", None),
            P("emb"),
            P("emb", None),
            P("emb", None),
            P("emb"),
            P("col", None),
            P("col", None),
            P(None, "col"),
            P(None, "col"),
            P("col"),
            P("col"),
            P("col"),
            P("col"),
        ),
        out_specs=(P("emb", "col"), P("emb", "col")),
        check_vma=False,
    )
```

profile of v0, /device:TPU:1, one launch (start us, length us, event | category | flops | bytes accessed | tf_op | source)
XLA Modules:
  0.0 443.1 jit_solution(14186168561972282029)
XLA Ops:
  5.1 20.6 %all-to-all-start = ((s32[128,1,2]{2,1,0:T(1,128)}), s32[128,1,2]{2,1,0:T(1,128)S(1)}, u32[]{:S(2)}, u32[]{:S(2)}) async-start(s32[128,1,2]{2,1,0:T(1,128)} %bitcast.3), calls=%async_computation | async-start | bytes 131072 | tf_op jit(solution)/shard_map/all_to_all | solution.py:63
  32.5 8.1 %all-to-all-done = s32[128,1,2]{2,1,0:T(1,128)S(1)} async-done(((s32[128,1,2]{2,1,0:T(1,128)}), s32[128,1,2]{2,1,0:T(1,128)S(1)}, u32[]{:S(2)}, u32[]{:S(2)}) %all-to-all-start) | async-done | bytes 1056 | tf_op jit(solution)/shard_map/all_to_all | solution.py:63
  40.6 8.1 %all-to-all-start.3 = ((s32[128,2,4]{2,1,0:T(2,128)}), s32[128,2,4]{2,1,0:T(2,128)S(1)}, u32[]{:S(2)}, u32[]{:S(2)}) async-start(s32[128,2,4]{2,1,0:T(2,128)} %reshape.163), calls=%async_computation.3 | async-start | bytes 262144 | tf_op jit(solution)/shard_map/all_to_all | solution.py:64
  48.7 5.0 %bitcast_select_fusion = bf16[128,2]{1,0:T(8,128)(2,1)S(1)} fusion(bf16[]{:T(256)} %bitcast.9, bf16[]{:T(256)} %bitcast.10, bf16[]{:T(256)} %bitcast.11, bf16[]{:T(256)} %bitcast.12, bf16[]{:T(256)} %bitcast.13, bf16[]{:T(256)} %bitcast.15, bf16[]{:T(256)} %bitcast.14, bf16[]{:T(256)} %bitcast.8, s32[128,2,1]{1,0,2:T(8,128)S(1)} %bitcast.67), kind=kLoop, calls=%fused_computation.60 | loop fusion | flops 4352 | bytes 1552 | tf_op jit(solution)/shard_map/jit(_take)/gather | solution.py:66
  54.7 11.4 %all-to-all-done.3 = s32[128,2,4]{2,1,0:T(2,128)S(1)} async-done(((s32[128,2,4]{2,1,0:T(2,128)}), s32[128,2,4]{2,1,0:T(2,128)S(1)}, u32[]{:S(2)}, u32[]{:S(2)}) %all-to-all-start.3) | async-done | bytes 4128 | tf_op jit(solution)/shard_map/all_to_all | solution.py:64
  66.1 6.9 %all-to-all-start.2 = ((bf16[128,1,2]{2,1,0:T(2,128)(2,1)}), bf16[128,1,2]{2,1,0:T(2,128)(2,1)S(1)}, u32[]{:S(2)}, u32[]{:S(2)}) async-start(bf16[128,1,2]{2,1,0:T(2,128)(2,1)} %copy.49), calls=%async_computation.2 | async-start | bytes 131072 | tf_op jit(solution)/shard_map/all_to_all | solution.py:70
  73.3 3.9 gather_fusion.3
  78.8 9.4 %all-to-all-done.2 = bf16[128,1,2]{2,1,0:T(2,128)(2,1)S(1)} async-done(((bf16[128,1,2]{2,1,0:T(2,128)(2,1)}), bf16[128,1,2]{2,1,0:T(2,128)(2,1)S(1)}, u32[]{:S(2)}, u32[]{:S(2)}) %all-to-all-start.2) | async-done | bytes 544 | tf_op jit(solution)/shard_map/all_to_all | solution.py:70
  88.2 7.8 %all-to-all-start.4 = ((bf16[128,2,4,256]{3,2,1,0:T(4,128)(2,1)}), bf16[128,2,4,256]{3,2,1,0:T(4,128)(2,1)}, u32[]{:S(2)}, u32[]{:S(2)}) async-start(bf16[128,2,4,256]{3,2,1,0:T(4,128)(2,1)} %broadcast_select_fusion.1), calls=%async_computation.4 | async-start | bytes 1048576 | tf_op jit(solution)/shard_map/all_to_all | solution.py:71
  98.0 2.7 reshape.172
  100.7 5.0 %broadcast_select_fusion = bf16[128,2,4096]{2,1,0:T(2,128)(2,1)} fusion(bf16[128,2,4096]{2,1,0:T(2,128)(2,1)} %reshape.172, pred[128,2]{1,0:T(8,128)(4,1)S(1)} %compare_and_fusion.1), kind=kLoop, calls=%fused_computation.12 | loop fusion | flops 1048576 | bytes 4194560 | tf_op jit(solution)/shard_map/jit(_take)/select_n | solution.py:65
  105.7 23.3 %all-to-all-done.4 = bf16[128,2,4,256]{3,2,1,0:T(4,128)(2,1)} async-done(((bf16[128,2,4,256]{3,2,1,0:T(4,128)(2,1)}), bf16[128,2,4,256]{3,2,1,0:T(4,128)(2,1)}, u32[]{:S(2)}, u32[]{:S(2)}) %all-to-all-start.4) | async-done | bytes 524320 | tf_op jit(solution)/shard_map/all_to_all | solution.py:71
  128.9 7.6 %all-to-all-start.1 = ((bf16[128,2,4096]{2,1,0:T(2,128)(2,1)}), bf16[128,2,4096]{2,1,0:T(2,128)(2,1)}, u32[]{:S(2)}, u32[]{:S(2)}) async-start(bf16[128,2,4096]{2,1,0:T(2,128)(2,1)} %broadcast_select_fusion), calls=%async_computation.1 | async-start | bytes 4194304 | tf_op jit(solution)/shard_map/all_to_all | solution.py:69
  142.1 93.2 %all-to-all-done.1 = bf16[128,2,4096]{2,1,0:T(2,128)(2,1)} async-done(((bf16[128,2,4096]{2,1,0:T(2,128)(2,1)}), bf16[128,2,4096]{2,1,0:T(2,128)(2,1)}, u32[]{:S(2)}, u32[]{:S(2)}) %all-to-all-start.1) | async-done | bytes 2097184 | tf_op jit(solution)/shard_map/all_to_all | solution.py:69
  235.3 2.7 reshape.158
  242.6 13.3 %psum.21 = bf16[128,128]{1,0:T(8,128)(2,1)S(1)} all-reduce(bf16[128,128]{1,0:T(8,128)(2,1)S(1)} %fusion.5), channel_id=1, replica_groups=mesh['emb'=128,'col'=4] {'col'}, use_global_device_ids=true, to_apply=%region_8.9 | all-reduce | flops 16384 | bytes 65536 | tf_op jit(solution)/shard_map/psum | solution.py:89
  259.9 12.5 %all-reduce = (bf16[128]{0:T(256)(128)(2,1)}, bf16[128,128]{1,0:T(8,128)(2,1)}) all-reduce(bf16[128]{0:T(256)(128)(2,1)} %add_convert_fusion, bf16[128,128]{1,0:T(8,128)(2,1)} %fusion.6), channel_id=1, replica_groups=mesh['emb'=128,'col'=4] {'col'}, use_global_device_ids=true, to_apply=%region_11.12 | all-reduce | flops 16512 | bytes 66048 | tf_op jit(solution)/shard_map/psum | solution.py:101
  277.1 3.5 scatter_custom_fusion.3
  282.6 16.5 %all-to-all-start.6 = ((bf16[128,2,4,256]{3,2,1,0:T(4,128)(2,1)}), bf16[128,2,4,256]{3,2,1,0:T(4,128)(2,1)}, u32[]{:S(2)}, u32[]{:S(2)}) async-start(bf16[128,2,4,256]{3,2,1,0:T(4,128)(2,1)} %reshape.168), calls=%async_computation.6 | async-start | bytes 1048576 | tf_op jit(solution)/shard_map/all_to_all | solution.py:128
  299.2 2.7 fusion
  301.9 3.4 scatter_custom_fusion.2
  307.9 24.0 %all-to-all-done.6 = bf16[128,2,4,256]{3,2,1,0:T(4,128)(2,1)} async-done(((bf16[128,2,4,256]{3,2,1,0:T(4,128)(2,1)}), bf16[128,2,4,256]{3,2,1,0:T(4,128)(2,1)}, u32[]{:S(2)}, u32[]{:S(2)}) %all-to-all-start.6) | async-done | bytes 524320 | tf_op jit(solution)/shard_map/all_to_all | solution.py:128
  332.0 7.2 %all-to-all-start.5 = ((bf16[128,2,4096]{2,1,0:T(2,128)(2,1)}), bf16[128,2,4096]{2,1,0:T(2,128)(2,1)S(1)}, u32[]{:S(2)}, u32[]{:S(2)}) async-start(bf16[128,2,4096]{2,1,0:T(2,128)(2,1)} %reshape.165), calls=%async_computation.5 | async-start | bytes 4194304 | tf_op jit(solution)/shard_map/all_to_all | solution.py:127
  344.6 93.6 %all-to-all-done.5 = bf16[128,2,4096]{2,1,0:T(2,128)(2,1)S(1)} async-done(((bf16[128,2,4096]{2,1,0:T(2,128)(2,1)}), bf16[128,2,4096]{2,1,0:T(2,128)(2,1)S(1)}, u32[]{:S(2)}, u32[]{:S(2)}) %all-to-all-start.5) | async-done | bytes 2097184 | tf_op jit(solution)/shard_map/all_to_all | solution.py:127
  (124 shorter events, 49.4 us)
Async XLA Ops:
  0.6 255.3 %copy-start = (bf16[128,4096]{1,0:T(8,128)(2,1)S(1)}, bf16[128,4096]{1,0:T(8,128)(2,1)}, u32[]{:S(2)}) copy-start(bf16[128,4096]{1,0:T(8,128)(2,1)} %param.26) | copy-start | bytes 3145732
  0.6 27.6 %copy-start.10 = (bf16[8]{0:T(256)(128)(2,1)S(1)}, bf16[8]{0:T(256)(128)(2,1)}, u32[]{:S(2)}) copy-start(bf16[8]{0:T(256)(128)(2,1)} %param.17) | copy-start | bytes 52
  0.7 28.3 %copy-start.17 = (s32[128,4]{0,1:T(4,128)S(1)}, s32[128,4]{0,1:T(4,128)}, u32[]{:S(2)}) copy-start(s32[128,4]{0,1:T(4,128)} %param.22) | copy-start | bytes 6148
  0.7 72.6 %copy-start.2 = (bf16[32,256]{1,0:T(8,128)(2,1)S(1)}, bf16[32,256]{1,0:T(8,128)(2,1)}, u32[]{:S(2)}) copy-start(bf16[32,256]{1,0:T(8,128)(2,1)} %param.18) | copy-start | bytes 49156
  3.2 135.3 %copy-start.18 = (s32[128,1]{0,1:T(1,128)}, s32[128,1]{0,1:T(1,128)S(1)}, u32[]{:S(2)}) copy-start(s32[128,1]{0,1:T(1,128)S(1)} %get-tuple-element.5) | copy-start | bytes 1540
  3.2 252.8 %copy-start.20 = (pred[128]{0:T(512)(128)(4,1)}, pred[128]{0:T(512)(128)(4,1)S(1)}, u32[]{:S(2)}) copy-start(pred[128]{0:T(512)(128)(4,1)S(1)} %get-tuple-element.4) | copy-start | bytes 388
  5.1 35.6 %all-to-all-start = ((s32[128,1,2]{2,1,0:T(1,128)}), s32[128,1,2]{2,1,0:T(1,128)S(1)}, u32[]{:S(2)}, u32[]{:S(2)}) async-start(s32[128,1,2]{2,1,0:T(1,128)} %bitcast.3), calls=%async_computation | async-start | bytes 131072 | tf_op jit(solution)/shard_map/all_to_all | solution.py:63
  28.2 108.7 %copy-start.14 = (s32[512,1]{0,1:T(1,128)}, s32[512,1]{0,1:T(1,128)S(1)}, u32[]{:S(2)}) copy-start(s32[512,1]{0,1:T(1,128)S(1)} %compare_select_fusion.9) | copy-start | bytes 6148
  40.6 25.5 %all-to-all-start.3 = ((s32[128,2,4]{2,1,0:T(2,128)}), s32[128,2,4]{2,1,0:T(2,128)S(1)}, u32[]{:S(2)}, u32[]{:S(2)}) async-start(s32[128,2,4]{2,1,0:T(2,128)} %reshape.163), calls=%async_computation.3 | async-start | bytes 262144 | tf_op jit(solution)/shard_map/all_to_all | solution.py:64
  66.1 22.1 %all-to-all-start.2 = ((bf16[128,1,2]{2,1,0:T(2,128)(2,1)}), bf16[128,1,2]{2,1,0:T(2,128)(2,1)S(1)}, u32[]{:S(2)}, u32[]{:S(2)}) async-start(bf16[128,1,2]{2,1,0:T(2,128)(2,1)} %copy.49), calls=%async_computation.2 | async-start | bytes 131072 | tf_op jit(solution)/shard_map/all_to_all | solution.py:70
  77.3 18.9 %copy-start.1 = (bf16[8,4096]{1,0:T(8,128)(2,1)S(1)}, bf16[8,4096]{1,0:T(8,128)(2,1)}, u32[]{:S(2)}) copy-start(bf16[8,4096]{1,0:T(8,128)(2,1)} %param.16) | copy-start | bytes 196612
  88.2 40.8 %all-to-all-start.4 = ((bf16[128,2,4,256]{3,2,1,0:T(4,128)(2,1)}), bf16[128,2,4,256]{3,2,1,0:T(4,128)(2,1)}, u32[]{:S(2)}, u32[]{:S(2)}) async-start(bf16[128,2,4,256]{3,2,1,0:T(4,128)(2,1)} %broadcast_select_fusion.1), calls=%async_computation.4 | async-start | bytes 1048576 | tf_op jit(solution)/shard_map/all_to_all | solution.py:71
  105.7 31.1 %copy-start.11 = (s32[128,4]{0,1:T(4,128)S(1)}, s32[128,4]{0,1:T(4,128)}, u32[]{:S(2)}) copy-start(s32[128,4]{0,1:T(4,128)} %param.21) | copy-start | bytes 6148
  128.9 106.4 %all-to-all-start.1 = ((bf16[128,2,4096]{2,1,0:T(2,128)(2,1)}), bf16[128,2,4096]{2,1,0:T(2,128)(2,1)}, u32[]{:S(2)}, u32[]{:S(2)}) async-start(bf16[128,2,4096]{2,1,0:T(2,128)(2,1)} %broadcast_select_fusion), calls=%async_computation.1 | async-start | bytes 4194304 | tf_op jit(solution)/shard_map/all_to_all | solution.py:69
  138.5 117.4 %copy-start.22 = (f32[128]{0:T(128)}, f32[128]{0:T(128)S(1)}, u32[]{:S(2)}) copy-start(f32[128]{0:T(128)S(1)} %bitcast_convert_fusion) | copy-start | bytes 1540
  240.3 15.7 %copy-start.3 = (bf16[128,4096]{1,0:T(8,128)(2,1)S(1)}, bf16[128,4096]{1,0:T(8,128)(2,1)}, u32[]{:S(2)}) copy-start(bf16[128,4096]{1,0:T(8,128)(2,1)} %gather_fusion.1) | copy-start | bytes 3145732
  240.3 15.7 %copy-start.12 = (f32[4096]{0:T(1024)S(1)}, f32[4096]{0:T(1024)}, u32[]{:S(2)}) copy-start(f32[4096]{0:T(1024)} %param.30) | copy-start | bytes 49156
  242.4 14.2 %copy-start.5 = (bf16[128,256]{1,0:T(8,128)(2,1)S(1)}, bf16[128,256]{1,0:T(8,128)(2,1)}, u32[]{:S(2)}) copy-start(bf16[128,256]{1,0:T(8,128)(2,1)} %param.27) | copy-start | bytes 196612
  242.5 14.9 %copy-start.19 = (f32[256]{0:T(256)S(1)}, f32[256]{0:T(256)}, u32[]{:S(2)}) copy-start(f32[256]{0:T(256)} %param.29) | copy-start | bytes 3076
  257.7 16.0 %copy-start.7 = (bf16[256,128]{1,0:T(8,128)(2,1)S(1)}, bf16[256,128]{1,0:T(8,128)(2,1)}, u32[]{:S(2)}) copy-start(bf16[256,128]{1,0:T(8,128)(2,1)} %param.25) | copy-start | bytes 196612
  274.6 24.5 %copy-start.8 = (bf16[128,128]{1,0:T(8,128)(2,1)S(1)}, bf16[128,128]{1,0:T(8,128)(2,1)}, u32[]{:S(2)}) copy-start(bf16[128,128]{1,0:T(8,128)(2,1)} %get-tuple-element.3) | copy-start | bytes 98308
  274.6 24.5 %copy-start.16 = (f32[128]{0:T(128)S(1)}, f32[128]{0:T(128)}, u32[]{:S(2)}) copy-start(f32[128]{0:T(128)} %copy-done.15) | copy-start | bytes 1540
  282.6 49.4 %all-to-all-start.6 = ((bf16[128,2,4,256]{3,2,1,0:T(4,128)(2,1)}), bf16[128,2,4,256]{3,2,1,0:T(4,128)(2,1)}, u32[]{:S(2)}, u32[]{:S(2)}) async-start(bf16[128,2,4,256]{3,2,1,0:T(4,128)(2,1)} %reshape.168), calls=%async_computation.6 | async-start | bytes 1048576 | tf_op jit(solution)/shard_map/all_to_all | solution.py:128
  332.0 106.3 %all-to-all-start.5 = ((bf16[128,2,4096]{2,1,0:T(2,128)(2,1)}), bf16[128,2,4096]{2,1,0:T(2,128)(2,1)S(1)}, u32[]{:S(2)}, u32[]{:S(2)}) async-start(bf16[128,2,4096]{2,1,0:T(2,128)(2,1)} %reshape.165), calls=%async_computation.5 | async-start | bytes 4194304 | tf_op jit(solution)/shard_map/all_to_all | solution.py:127
  (6 other events, 21.5 us)
where the time goes:
time: 445 us; the launch traced here: 443 us
  waiting for transfers between devices  263 us (59%)
  starting transfers between devices  74.6 us (17%)
  local copies, waits for them, and re-layouts  46.8 us (11%)
  blocking collectives  25.8 us (6%)
  other arithmetic  17.9 us (4%)
  matrix products  13.7 us (3%)
    all_to_all x1, waiting for transfers between devices, body(): lax.all_to_all(user_send, 'emb', split_axis=0, concat_axis=0, tiled=True)  93.6 us
    all_to_all x1, waiting for transfers between devices, body(): lax.all_to_all(found_rows, 'emb', split_axis=0, concat_axis=0, tiled=True)  93.2 us
    all_to_all x1, waiting for transfers between devices, body(): lax.all_to_all(item_send, 'emb', split_axis=0, concat_axis=0, tiled=True)  24 us
    all_to_all x1, waiting for transfers between devices, body(): lax.all_to_all(found_items, 'emb', split_axis=0, concat_axis=0, tiled=True)  23.3 us
    all_to_all x1, starting transfers between devices, body(): lax.all_to_all(user_want, 'emb', split_axis=0, concat_axis=0, tiled=True)  20.6 us
    all_to_all x1, starting transfers between devices, body(): lax.all_to_all(item_send, 'emb', split_axis=0, concat_axis=0, tiled=True)  16.5 us
    psum x1, blocking collectives, body(): lowrank = lax.psum(low_part.astype(jnp.bfloat16), 'col')  13.3 us
    psum x1, blocking collectives, body(): lax.psum(logit_part.astype(jnp.bfloat16), 'col').astype(jnp.float32)  12.5 us
  transfers between devices with their start and end apart: 7, of which 7 were waited for; matrix products, arithmetic and copies ran while one was open for 11% of the time, Pallas kernels for 0%

commit v1 on v0

v1 whole, which is shorter than its diff:
```python
import jax
import jax.numpy as jnp
from jax import lax
from jax.experimental import pallas as pl
from jax.experimental.pallas import tpu as pltpu
from jax.sharding import Mesh, PartitionSpec as P

loss_scale = 128.0
bf16 = jnp.bfloat16
f32 = jnp.float32
i32 = jnp.int32
EMB = ("y", "z", "c")
BLOCK = ("y", "c", "x")
LANES = 128
FRONT = 24


def dot(a, b, ca=1, cb=0):
    return lax.dot_general(a, b, (((ca,), (cb,)), ((), ())), preferred_element_type=f32)


def iota(shape, axis):
    return lax.broadcasted_iota(i32, shape, axis)


def roll(value, shift):
    shift = shift % LANES
    return pltpu.roll(value, shift, 1) if shift else value


def column(row, rows, first):
    hit = iota((rows, LANES), 1) == iota((rows, LANES), 0) + first
    return jnp.sum(jnp.where(hit, row, 0.0), axis=1, keepdims=True)


def pack(full, extra):
    held = full.shape[0]
    lane = iota((held, LANES), 1)
    line = jnp.sum(jnp.where(lane == iota((held, LANES), 0) + 64, extra, 0.0), axis=0, keepdims=True)
    tail = jnp.where(iota((2 * FRONT - held, LANES), 0) == 0, line, 0.0)
    right = jnp.concatenate([roll(full[FRONT:], 64), tail], axis=0)
    return jnp.where(lane[:FRONT] < 64, full[:FRONT], right)


def unpack(block, held):
    lane = iota((held, LANES), 1)
    full = jnp.concatenate([block, roll(block[: held - FRONT], 64)], axis=0)
    extra = column(block[held - FRONT : held - FRONT + 1], held, 64)
    return jnp.where(lane < 64, full, jnp.where(lane == 64, extra, 0.0))


def plane_at(cores):
    return lax.axis_index("y") * cores + lax.axis_index("c")


def row_parts(rows, enter, leave, bias, head):
    wide = rows.astype(f32)
    low = dot(rows, enter)
    carry = dot((wide * head).astype(bf16), leave, 1, 1)
    return low, carry, jnp.sum(head * (wide * bias + wide), axis=1, keepdims=True)


def parts_kernel(
    cols, cores, table_u, scale, table_i, owner_u, row_u, owner_i, row_i, enter_u, enter_i, leave_u, leave_i,
    bias_u, bias_i, head_u, head_i, send, names,
):
    users = table_u.shape[0]
    part = enter_u.shape[1] // cols
    scales = scale[...].astype(f32)
    eye = iota((users, users), 0) == iota((users, users), 1)
    scales = jnp.sum(jnp.where(eye, scales, 0.0), axis=1, keepdims=True)
    rows = (table_u[...].astype(f32) * scales).astype(bf16)
    low_u, carry_u, line_u = row_parts(rows, enter_u[...], leave_u[...], bias_u[...], head_u[...])
    low_i, carry_i, line_i = row_parts(table_i[...], enter_i[...], leave_i[...], bias_i[...], head_i[...])
    low = jnp.concatenate([low_u, low_i], axis=0)
    carry = jnp.concatenate([carry_u, carry_i], axis=0)
    line = jnp.concatenate([line_u, line_i], axis=0)
    lane = iota(low.shape, 1)
    packed = []
    for x in range(cols):
        full = jnp.where(lane < part, roll(low, -part * x), roll(carry, part - part * x))
        packed.append(pack(full, line).astype(bf16))
    lists = owner_i.shape[0]
    fill = jnp.zeros((FRONT - 2 * lists - 2, LANES), i32)
    idx = jnp.concatenate([owner_u[...], row_u[...], owner_i[...], row_i[...], fill], axis=0)
    idx = idx.astype(f32).astype(bf16)
    names[...] = idx
    mine = plane_at(cores)
    for p in range(send.shape[0]):
        send[p] = jnp.where(mine == p // cols, packed[p % cols], idx)


def share_kernel(cols, cores, came, send):
    mine = plane_at(cores)
    total = came[mine * cols].astype(f32)
    for x in range(1, cols):
        total = total + came[mine * cols + x].astype(f32)
    total = total.astype(bf16)
    for z in range(send.shape[0]):
        send[z] = total


def pick_kernel(cols, cores, depth, users, held, lists, came, names, pick, pick_t):
    mine = plane_at(cores)
    peers = came.shape[0] // cols
    imps, span = LANES, depth * held
    keys = []
    for p in range(peers):
        idx = jnp.where(mine == p, names[...], came[p * cols]).astype(f32).astype(i32)
        owner = jnp.concatenate([idx[0:1], idx[2 : 2 + lists]], axis=0)
        row = jnp.concatenate([idx[1:2], idx[2 + lists : 2 + 2 * lists] + users], axis=0)
        chip = owner // cores
        at = (chip // depth) * cores + owner % cores
        key = jnp.where(at == mine, (chip % depth) * held + row, -1)
        keys.append(jnp.concatenate([key, jnp.full((8 - key.shape[0], imps), -1, i32)], axis=0))
    ids = iota((span, imps), 0)
    for p in range(peers):
        hit = ids == keys[p][0:1]
        for j in range(1, 1 + lists):
            hit = hit | (ids == keys[p][j : j + 1])
        pick_t[:, p * imps : (p + 1) * imps] = jnp.where(hit, 1.0, 0.0).astype(bf16)
    every = jnp.concatenate(keys, axis=0).astype(f32)
    every = jnp.concatenate([every, jnp.zeros((LANES - every.shape[0], LANES), f32)], axis=0)
    every = jnp.transpose(every).astype(i32)
    ids = iota((imps, span), 1)
    for p in range(peers):
        hit = ids == every[:, 8 * p : 8 * p + 1]
        for j in range(1, 1 + lists):
            hit = hit | (ids == every[:, 8 * p + j : 8 * p + j + 1])
        pick[p * imps : (p + 1) * imps, :] = jnp.where(hit, 1.0, 0.0).astype(bf16)


def fetch_kernel(held, came, pick, send):
    table = [unpack(came[z].astype(f32), held) for z in range(came.shape[0])]
    table = jnp.concatenate(table, axis=0).astype(bf16)
    send[...] = dot(pick[...], table).astype(bf16)


def loss_kernel(cols, part, came, labels, send):
    own = came.shape[1]
    peers = came.shape[0] // cols
    lane = iota((own, LANES), 1)
    sums = []
    logits = None
    for x in range(cols):
        total = came[x].astype(f32)
        for p in range(1, peers):
            total = total + came[p * cols + x].astype(f32)
        sums.append(total)
        term = jnp.where(lane < part, total * roll(total, -part), 0.0)
        if x == 0:
            term = term + jnp.where(lane == 2 * part, total, 0.0)
        logits = term if logits is None else logits + term
    logits = jnp.sum(logits, axis=1, keepdims=True)
    target = column(labels[...], own, lax.axis_index("x") * own)
    grad = loss_scale * (1.0 / (1.0 + jnp.exp(-logits)) - target)
    for x in range(cols):
        back = (grad * jnp.where(lane == 2 * part, 1.0, sums[x])).astype(bf16)
        for p in range(peers):
            send[p * cols + x] = back


def back_kernel(held, came, pick_t, send):
    sums = dot(pick_t[...], came[...])
    for z in range(send.shape[0]):
        full = sums[z * held : (z + 1) * held]
        send[z] = pack(full, full[:, 64:65]).astype(bf16)


def total_kernel(came, send):
    total = came[0].astype(f32)
    for z in range(1, came.shape[0]):
        total = total + came[z].astype(f32)
    total = total.astype(bf16)
    for x in range(send.shape[0]):
        send[x] = total


def grad_kernel(
    part, users, held, came, enter_u, enter_i, leave_u, leave_i, bias_u, bias_i, head_u, head_i, out_u, out_i
):
    lane = iota((held, LANES), 1)
    low = carry = jnp.zeros((held, LANES), f32)
    for x in range(came.shape[0]):
        full = unpack(came[x].astype(f32), held)
        if x == 0:
            line = full[:, 64:65]
        here = (lane >= part * x) & (lane < part * (x + 1))
        low = jnp.where(here, roll(full, part * x), low)
        carry = jnp.where(here, roll(full, part * x - part), carry)
    low, carry = low.astype(bf16), carry.astype(bf16)
    for out, a, b, enter, leave, bias, head in (
        (out_u, 0, users, enter_u, leave_u, bias_u, head_u),
        (out_i, users, held, enter_i, leave_i, bias_i, head_i),
    ):
        hidden = dot(low[a:b], leave[...])
        out[...] = head[...] * (hidden + line[a:b] * (bias[...] + 1.0)) + dot(carry[a:b], enter[...], 1, 1)


def call(kernel, outs, flops, bytes_accessed, *args, fetch=False):
    many = isinstance(outs, list)
    spec = pl.BlockSpec(memory_space=pltpu.VMEM)
    if fetch:
        return pl.pallas_call(
            kernel,
            out_shape=outs,
            grid=(1,),
            in_specs=[pl.BlockSpec(a.shape, lambda i: (0, 0)) for a in args],
            out_specs=[spec] * len(outs) if many else spec,
            compiler_params=pltpu.CompilerParams(vmem_limit_bytes=60 * 1024 * 1024),
            cost_estimate=pl.CostEstimate(flops=flops, bytes_accessed=bytes_accessed, transcendentals=0),
        )(*args)
    return pl.pallas_call(
        kernel,
        out_shape=outs,
        in_specs=[spec] * len(args),
        out_specs=[spec] * len(outs) if many else spec,
        compiler_params=pltpu.CompilerParams(vmem_limit_bytes=40 * 1024 * 1024),
        cost_estimate=pl.CostEstimate(flops=flops, bytes_accessed=bytes_accessed, transcendentals=0),
    )(*args)


def swap(value, axes):
    return lax.all_to_all(value, axes, split_axis=0, concat_axis=0, tiled=True)


def body(
    user_table,
    user_scale,
    item_table,
    user_owner,
    user_row,
    item_owner,
    item_row,
    labels,
    enter_user,
    enter_item,
    leave_user,
    leave_item,
    bias_user,
    bias_item,
    head_user,
    head_item,
):
    cols, depth, cores = lax.axis_size("x"), lax.axis_size("z"), lax.axis_size("c")
    peers = lax.axis_size("y") * cores
    users, items = user_table.shape[0], item_table.shape[0]
    imps, lists = item_row.shape
    part = enter_user.shape[1] // cols
    held = users + items
    span = depth * held
    own = imps // cols
    shape = jax.ShapeDtypeStruct
    weights = (enter_user, enter_item, leave_user, leave_item) + tuple(
        v[None] for v in (bias_user, bias_item, head_user, head_item)
    )

    send, names = call(
        lambda *refs: parts_kernel(cols, cores, *refs),
        [shape((peers * cols, FRONT, LANES), bf16), shape((FRONT, LANES), bf16)],
        20_000_000, 2_500_000,
        user_table, user_scale[None], item_table, user_owner.T, user_row[None], item_owner.T, item_row.T, *weights, fetch=True,
    )
    came = swap(send, BLOCK)
    send = call(
        lambda *refs: share_kernel(cols, cores, *refs), shape((depth, FRONT, LANES), bf16), 100_000, 200_000, came
    )
    table = swap(send, "z")
    pick, pick_t = call(
        lambda *refs: pick_kernel(cols, cores, depth, users, held, lists, *refs),
        [shape((peers * imps, span), bf16), shape((span, peers * imps), bf16)],
        100_000_000, 10_000_000,
        came, names,
    )
    send = call(
        lambda *refs: fetch_kernel(held, *refs), shape((peers * imps, LANES), bf16), 200_000_000, 1_500_000, table, pick
    )
    came = swap(send.reshape(peers * cols, own, LANES), BLOCK)
    send = call(
        lambda *refs: loss_kernel(cols, part, *refs),
        shape((peers * cols, own, LANES), bf16), 1_000_000, 500_000,
        came, labels[None],
    )
    came = swap(send, BLOCK)
    send = call(
        lambda *refs: back_kernel(held, *refs),
        shape((depth, FRONT, LANES), bf16), 200_000_000, 1_500_000,
        came.reshape(peers * imps, LANES), pick_t,
    )
    came = swap(send, "z")
    send = call(total_kernel, shape((cols, FRONT, LANES), bf16), 100_000, 200_000, came)
    came = swap(send, "x")
    user_grad, item_grad = call(
        lambda *refs: grad_kernel(part, users, held, *refs),
        [shape(user_table.shape, f32), shape(item_table.shape, f32)],
        20_000_000, 2_500_000,
        came, *weights,
    )
    return (user_grad, item_grad)


def solution(mesh):
    cols = mesh.shape["col"]
    cells = mesh.devices.reshape(-1, 16, 2, cols)
    fine = Mesh(cells, ("y", "z", "c", "x"))
    return jax.shard_map(
        body,
        mesh=fine,
        in_specs=(
            P(EMB, "x"),
            P(EMB),
            P(EMB, "x"),
            P(EMB, None),
            P(EMB),
            P(EMB, None),
            P(EMB, None),
            P(EMB),
            P("x", None),
            P("x", None),
            P(None, "x"),
            P(None, "x"),
            P("x"),
            P("x"),
            P("x"),
            P("x"),
        ),
        out_specs=(P(EMB, "x"), P(EMB, "x")),
        check_vma=False,
    )
```

time: 445 us -> 102 us (0.23)
  waiting for transfers between devices: 263 us -> 7.35 us
  starting transfers between devices: 74.6 us -> 13 us
  local copies, waits for them, and re-layouts: 46.8 us -> 0.75 us
  blocking collectives: 25.8 us -> 67.7 us
  other arithmetic: 17.9 us -> 0 us
  matrix products: 13.7 us -> 0 us
  Pallas kernels: 0 us -> 10.5 us
    all_to_all x7 -> x1, waiting for transfers between devices: 263 us -> 7.35 us  [swap(): return lax.all_to_all(value, axes, split_axis=0, concat_axis=0, tiled=True)]
    all_to_all x0 -> x5, blocking collectives: none -> 67.7 us  [swap(): return lax.all_to_all(value, axes, split_axis=0, concat_axis=0, tiled=True)]
    all_to_all x7 -> x1, starting transfers between devices: 74.6 us -> 13 us  [swap(): return lax.all_to_all(value, axes, split_axis=0, concat_axis=0, tiled=True)]
    psum x2 -> x0, blocking collectives: 25.8 us -> none  [the longest x1 13.3 us: body(): lowrank = lax.psum(low_part.astype(jnp.bfloat16), 'col')]
    reshape x11 -> x0, local copies, waits for them, and re-layouts: 15.7 us -> none  [the longest x1 2.74 us: body(): got_rows.reshape(owners * user_cap, user_width)]
    gather x10 -> x0, local copies, waits for them, and re-layouts: 14.8 us -> none  [the longest x2 4.51 us: body(): found_rows = jnp.take(user_table, user_ask, axis=0)]
    dot_general x10 -> x0, matrix products: 13.7 us -> none  [the longest x4 5.01 us: contract(): lax.dot_general(matrix, factor, (((1,), (1,)), ((), ())), preferred_eleme...]
    pallas_call x0 -> x8, Pallas kernels: none -> 10.5 us  [the longest x7 7.42 us: call(): pl.pallas_call(kernel, out_shape=outs, in_specs=[spec] * len(args), out_s...]
  transfers between devices with their start and end apart: 7 -> 1, of which waited for: 7 -> 1; matrix products, arithmetic and copies ran while one was open for 11% -> 0% of each run, Pallas kernels for 0% -> 4%
where the time goes in v1:
time: 102 us; the launch traced here: 100 us
  blocking collectives  67.7 us (66%)
  starting transfers between devices  13 us (13%)
  Pallas kernels  10.5 us (10%)
  waiting for transfers between devices  7.35 us (7%)
    all_to_all x5, blocking collectives, swap(): return lax.all_to_all(value, axes, split_axis=0, concat_axis=0, tiled=True)  67.7 us
    all_to_all x1, starting transfers between devices, swap(): return lax.all_to_all(value, axes, split_axis=0, concat_axis=0, tiled=True)  13 us
    pallas_call x7, Pallas kernels, call(): pl.pallas_call(kernel, out_shape=outs, in_specs=[spec] * len(args), out_s...  7.42 us
    all_to_all x1, waiting for transfers between devices, swap(): return lax.all_to_all(value, axes, split_axis=0, concat_axis=0, tiled=True)  7.35 us
    pallas_call x1, Pallas kernels, call(): pl.pallas_call(kernel, out_shape=outs, grid=(1,), in_specs=[pl.BlockSpec(...  3.08 us
  transfers between devices with their start and end apart: 1, of which 1 were waited for; matrix products, arithmetic and copies ran while one was open for 0% of the time, Pallas kernels for 4%

profile of v1, /device:TPU:1, one launch (start us, length us, event | category | flops | bytes accessed | tf_op | source)
XLA Modules:
  0.0 100.1 jit_solution(9796131266223066919)
XLA Ops:
  0.6 3.1 %shard_map.167 = (bf16[32,24,128]{2,1,0:T(8,128)(2,1)}, bf16[24,128]{1,0:T(8,128)(2,1)}) custom-call(bf16[8,4096]{1,0:T(8,128)(2,1)} %refs_0_.1, bf16[1,8]{1,0:T(2,128)(2,1)} %bitcast.25, bf16[32,256]{1,0:T(8,128)(2,1)} %refs_2_.2, s32[1,128]{1,0:T(1,128)} %bitcast.26, s32[1,128]{1,0:T(1,128)} %bitcast.27, s32[4,128]{1,0:T(4,128)} %bitcast.23, ...), custom_call_target="tpu_custom_call" | custom-call | flops 20000000 | bytes 2500000 | tf_op jit(solution)/shard_map/pallas_call | solution.py:204
  3.7 18.8 %all_to_all.30.refs_0_ = bf16[32,24,128]{2,1,0:T(8,128)(2,1)S(1)} all-to-all(bf16[32,24,128]{2,1,0:T(8,128)(2,1)} %get-tuple-element.6), channel_id=1, replica_groups=mesh['y'=4,'z'=16,'c'=2,'x'=4] {'y','c','x'}, dimensions={0} | all-to-all | bytes 393216 | tf_op jit(solution)/shard_map/all_to_all | solution.py:224
  22.5 0.7 shard_map.168
  23.1 13.0 %all-to-all-start.1 = ((bf16[16,24,128]{2,1,0:T(8,128)(2,1)}), bf16[16,24,128]{2,1,0:T(8,128)(2,1)S(1)}, u32[]{:S(2)}, u32[]{:S(2)}) async-start(bf16[16,24,128]{2,1,0:T(8,128)(2,1)} %shard_map.168), calls=%async_computation.1 | async-start | bytes 196608 | tf_op jit(solution)/shard_map/all_to_all | solution.py:224
  36.1 0.0 copy-start.8
  36.1 0.0 copy-start.9
  36.2 0.7 copy-done.9
  36.8 3.9 %shard_map.169 = (bf16[1024,640]{1,0:T(8,128)(2,1)S(1)}, bf16[640,1024]{1,0:T(8,128)(2,1)S(1)}) custom-call(bf16[32,24,128]{2,1,0:T(8,128)(2,1)S(1)} %all_to_all.30.refs_0_, bf16[24,128]{1,0:T(8,128)(2,1)S(1)} %copy-done.9), custom_call_target="tpu_custom_call" | custom-call | flops 100000000 | bytes 10000000 | tf_op jit(solution)/shard_map/pallas_call | solution.py:213
  40.8 7.3 %all-to-all-done.1.refs_0_ = bf16[16,24,128]{2,1,0:T(8,128)(2,1)S(1)} async-done(((bf16[16,24,128]{2,1,0:T(8,128)(2,1)}), bf16[16,24,128]{2,1,0:T(8,128)(2,1)S(1)}, u32[]{:S(2)}, u32[]{:S(2)}) %all-to-all-start.1) | async-done | bytes 98336 | tf_op jit(solution)/shard_map/all_to_all | solution.py:224
  48.1 0.7 shard_map.170
  48.8 14.3 %all_to_all.31.refs_0_ = bf16[32,32,128]{2,1,0:T(8,128)(2,1)S(1)} all-to-all(bf16[32,32,128]{2,1,0:T(8,128)(2,1)S(1)} %bitcast.13), channel_id=1, replica_groups=mesh['y'=4,'z'=16,'c'=2,'x'=4] {'y','c','x'}, dimensions={0} | all-to-all | bytes 524288 | tf_op jit(solution)/shard_map/all_to_all | solution.py:224
  63.2 0.2 shard_map.171
  63.4 0.0 copy-start
  63.4 0.0 copy-start.1
  63.4 0.0 copy-start.2
  63.4 0.0 copy-start.3
  63.4 0.0 copy-start.4
  63.4 0.0 copy-start.5
  63.5 0.0 copy-start.6
  63.5 12.9 %all_to_all.32 = bf16[32,32,128]{2,1,0:T(8,128)(2,1)S(1)} all-to-all(bf16[32,32,128]{2,1,0:T(8,128)(2,1)S(1)} %shard_map.171), channel_id=1, replica_groups=mesh['y'=4,'z'=16,'c'=2,'x'=4] {'y','c','x'}, dimensions={0} | all-to-all | bytes 524288 | tf_op jit(solution)/shard_map/all_to_all | solution.py:224
  76.4 0.6 shard_map.172
  77.0 15.1 %all_to_all.33.came = bf16[16,24,128]{2,1,0:T(8,128)(2,1)S(1)} all-to-all(bf16[16,24,128]{2,1,0:T(8,128)(2,1)S(1)} %shard_map.172), channel_id=1, replica_groups=mesh['y'=4,'z'=16,'c'=2,'x'=4] {'z'}, dimensions={0} | all-to-all | bytes 196608 | tf_op jit(solution)/shard_map/all_to_all | solution.py:224
  92.1 6.6 %all_to_all.34.refs_0_ = bf16[4,24,128]{2,1,0:T(8,128)(2,1)S(1)} all-to-all(bf16[4,24,128]{2,1,0:T(8,128)(2,1)S(1)} %shard_map.173), channel_id=1, replica_groups=mesh['y'=4,'z'=16,'c'=2,'x'=4] {'x'}, dimensions={0} | all-to-all | bytes 49152 | tf_op jit(solution)/shard_map/all_to_all | solution.py:224
  98.8 1.3 %shard_map.174 = (f32[8,4096]{1,0:T(8,128)}, f32[32,256]{1,0:T(8,128)}) custom-call(bf16[4,24,128]{2,1,0:T(8,128)(2,1)S(1)} %all_to_all.34.refs_0_, bf16[4096,128]{1,0:T(8,128)(2,1)S(1)} %copy-done, bf16[256,128]{1,0:T(8,128)(2,1)S(1)} %copy-done.2, bf16[128,4096]{1,0:T(8,128)(2,1)S(1)} %copy-done.1, bf16[128,256]{1,0:T(8,128)(2,1)S(1)} %copy-done.3, ...), custom_call_target="tpu_custom_call" | custom-call | flops 20000000 | bytes 2500000 | tf_op jit(solution)/shard_map/pallas_call | solution.py:213
  (11 shorter events, 0.0 us)
Async XLA Ops:
  23.1 25.0 %all-to-all-start.1 = ((bf16[16,24,128]{2,1,0:T(8,128)(2,1)}), bf16[16,24,128]{2,1,0:T(8,128)(2,1)S(1)}, u32[]{:S(2)}, u32[]{:S(2)}) async-start(bf16[16,24,128]{2,1,0:T(8,128)(2,1)} %shard_map.168), calls=%async_computation.1 | async-start | bytes 196608 | tf_op jit(solution)/shard_map/all_to_all | solution.py:224
  36.1 27.0 %copy-start.8 = (f32[128]{0:T(128)S(1)}, f32[128]{0:T(128)}, u32[]{:S(2)}) copy-start(f32[128]{0:T(128)} %param.23) | copy-start | bytes 1540
  36.1 0.7 copy-start.9
  63.4 35.3 %copy-start = (bf16[4096,128]{1,0:T(8,128)(2,1)S(1)}, bf16[4096,128]{1,0:T(8,128)(2,1)}, u32[]{:S(2)}) copy-start(bf16[4096,128]{1,0:T(8,128)(2,1)} %refs_1_.1) | copy-start | bytes 3145732
  63.4 35.3 %copy-start.1 = (bf16[128,4096]{1,0:T(8,128)(2,1)S(1)}, bf16[128,4096]{1,0:T(8,128)(2,1)}, u32[]{:S(2)}) copy-start(bf16[128,4096]{1,0:T(8,128)(2,1)} %refs_3_.1) | copy-start | bytes 3145732
  63.4 35.3 %copy-start.2 = (bf16[256,128]{1,0:T(8,128)(2,1)S(1)}, bf16[256,128]{1,0:T(8,128)(2,1)}, u32[]{:S(2)}) copy-start(bf16[256,128]{1,0:T(8,128)(2,1)} %refs_2_.3) | copy-start | bytes 196612
  63.4 35.3 %copy-start.3 = (bf16[128,256]{1,0:T(8,128)(2,1)S(1)}, bf16[128,256]{1,0:T(8,128)(2,1)}, u32[]{:S(2)}) copy-start(bf16[128,256]{1,0:T(8,128)(2,1)} %refs_4_.1) | copy-start | bytes 196612
  63.4 35.3 %copy-start.4 = (f32[4096]{0:T(1024)S(1)}, f32[4096]{0:T(1024)}, u32[]{:S(2)}) copy-start(f32[4096]{0:T(1024)} %param.28) | copy-start | bytes 49156
  63.4 35.3 %copy-start.5 = (f32[4096]{0:T(1024)S(1)}, f32[4096]{0:T(1024)}, u32[]{:S(2)}) copy-start(f32[4096]{0:T(1024)} %param.30) | copy-start | bytes 49156
  63.5 35.3 %copy-start.6 = (f32[256]{0:T(256)S(1)}, f32[256]{0:T(256)}, u32[]{:S(2)}) copy-start(f32[256]{0:T(256)} %param.29) | copy-start | bytes 3076
  63.5 35.3 %copy-start.7 = (f32[256]{0:T(256)S(1)}, f32[256]{0:T(256)}, u32[]{:S(2)}) copy-start(f32[256]{0:T(256)} %param.31) | copy-start | bytes 3076

commit v2 on v1

--- a/solution.py
+++ b/solution.py
@@ -10,7 +10,7 @@
 f32 = jnp.float32
 i32 = jnp.int32
 EMB = ("y", "z", "c")
-BLOCK = ("y", "c", "x")
+BLOCK = ("y", "x")
 LANES = 128
 FRONT = 24
 
@@ -28,8 +28,9 @@
     return pltpu.roll(value, shift, 1) if shift else value
 
 
-def column(row, rows, first):
-    hit = iota((rows, LANES), 1) == iota((rows, LANES), 0) + first
+def column(row, rows, first=0):
+    wide = (rows, row.shape[1])
+    hit = iota(wide, 1) == iota(wide, 0) + first
     return jnp.sum(jnp.where(hit, row, 0.0), axis=1, keepdims=True)
 
 
@@ -49,10 +50,6 @@
     return jnp.where(lane < 64, full, jnp.where(lane == 64, extra, 0.0))
 
 
-def plane_at(cores):
-    return lax.axis_index("y") * cores + lax.axis_index("c")
-
-
 def row_parts(rows, enter, leave, bias, head):
     wide = rows.astype(f32)
     low = dot(rows, enter)
@@ -60,15 +57,18 @@
     return low, carry, jnp.sum(head * (wide * bias + wide), axis=1, keepdims=True)
 
 
+def turn(column):
+    eye = iota((LANES, LANES), 0) == iota((LANES, LANES), 1)
+    return jnp.sum(jnp.where(eye, column, 0.0), axis=0, keepdims=True)
+
+
 def parts_kernel(
-    cols, cores, table_u, scale, table_i, owner_u, row_u, owner_i, row_i, enter_u, enter_i, leave_u, leave_i,
+    cols, table_u, scale, table_i, owner_u, row_u, owner_i, row_i, labels, enter_u, enter_i, leave_u, leave_i,
     bias_u, bias_i, head_u, head_i, send, names,
 ):
     users = table_u.shape[0]
     part = enter_u.shape[1] // cols
-    scales = scale[...].astype(f32)
-    eye = iota((users, users), 0) == iota((users, users), 1)
-    scales = jnp.sum(jnp.where(eye, scales, 0.0), axis=1, keepdims=True)
+    scales = column(scale[...].astype(f32), users)
     rows = (table_u[...].astype(f32) * scales).astype(bf16)
     low_u, carry_u, line_u = row_parts(rows, enter_u[...], leave_u[...], bias_u[...], head_u[...])
     low_i, carry_i, line_i = row_parts(table_i[...], enter_i[...], leave_i[...], bias_i[...], head_i[...])
@@ -80,18 +80,23 @@
     for x in range(cols):
         full = jnp.where(lane < part, roll(low, -part * x), roll(carry, part - part * x))
         packed.append(pack(full, line).astype(bf16))
-    lists = owner_i.shape[0]
-    fill = jnp.zeros((FRONT - 2 * lists - 2, LANES), i32)
-    idx = jnp.concatenate([owner_u[...], row_u[...], owner_i[...], row_i[...], fill], axis=0)
-    idx = idx.astype(f32).astype(bf16)
+    names_now = [owner_u[...], row_u[...], owner_i[...], row_i[...]]
+    rest = labels[...]
+    targets = []
+    for _ in range(3):
+        piece = rest.astype(bf16).astype(f32)
+        targets.append(piece)
+        rest = rest - piece
+    idx = jnp.concatenate([v.astype(f32) for v in names_now] + targets, axis=0)
+    idx = jnp.concatenate([idx, jnp.zeros((FRONT - idx.shape[0], LANES), f32)], axis=0).astype(bf16)
     names[...] = idx
-    mine = plane_at(cores)
+    mine = lax.axis_index("y")
     for p in range(send.shape[0]):
         send[p] = jnp.where(mine == p // cols, packed[p % cols], idx)
 
 
-def share_kernel(cols, cores, came, send):
-    mine = plane_at(cores)
+def share_kernel(cols, came, send):
+    mine = lax.axis_index("y")
     total = came[mine * cols].astype(f32)
     for x in range(1, cols):
         total = total + came[mine * cols + x].astype(f32)
@@ -100,19 +105,23 @@
         send[z] = total
 
 
-def pick_kernel(cols, cores, depth, users, held, lists, came, names, pick, pick_t):
-    mine = plane_at(cores)
+def pick_kernel(cols, cores, depth, users, held, lists, came, names, pick, pick_t, labels):
+    mine, core = lax.axis_index("y"), lax.axis_index("c")
     peers = came.shape[0] // cols
-    imps, span = LANES, depth * held
-    keys = []
+    imps, span = LANES, cores * depth * held
+    keys, targets = [], []
     for p in range(peers):
-        idx = jnp.where(mine == p, names[...], came[p * cols]).astype(f32).astype(i32)
+        block = jnp.where(mine == p, names[...], came[p * cols]).astype(f32)
+        idx = block.astype(i32)
         owner = jnp.concatenate([idx[0:1], idx[2 : 2 + lists]], axis=0)
         row = jnp.concatenate([idx[1:2], idx[2 + lists : 2 + 2 * lists] + users], axis=0)
         chip = owner // cores
-        at = (chip // depth) * cores + owner % cores
-        key = jnp.where(at == mine, (chip % depth) * held + row, -1)
+        side = jnp.where(owner % cores == core, 0, depth)
+        key = jnp.where(chip // depth == mine, (side + chip % depth) * held + row, -1)
         keys.append(jnp.concatenate([key, jnp.full((8 - key.shape[0], imps), -1, i32)], axis=0))
+        first = 2 + 2 * lists
+        targets.append((block[first : first + 1] + block[first + 1 : first + 2]) + block[first + 2 : first + 3])
+    labels[...] = jnp.concatenate(targets + [jnp.zeros((8 - peers, LANES), f32)], axis=0)
     ids = iota((span, imps), 0)
     for p in range(peers):
         hit = ids == keys[p][0:1]
@@ -130,41 +139,67 @@
         pick[p * imps : (p + 1) * imps, :] = jnp.where(hit, 1.0, 0.0).astype(bf16)
 
 
-def fetch_kernel(held, came, pick, send):
-    table = [unpack(came[z].astype(f32), held) for z in range(came.shape[0])]
+def fetch_kernel(held, mine, other, pick, send):
+    table = [unpack(side[z].astype(f32), held) for side in (mine, other) for z in range(mine.shape[0])]
     table = jnp.concatenate(table, axis=0).astype(bf16)
-    send[...] = dot(pick[...], table).astype(bf16)
-
-
-def loss_kernel(cols, part, came, labels, send):
-    own = came.shape[1]
-    peers = came.shape[0] // cols
-    lane = iota((own, LANES), 1)
-    sums = []
-    logits = None
-    for x in range(cols):
-        total = came[x].astype(f32)
-        for p in range(1, peers):
-            total = total + came[p * cols + x].astype(f32)
-        sums.append(total)
-        term = jnp.where(lane < part, total * roll(total, -part), 0.0)
-        if x == 0:
-            term = term + jnp.where(lane == 2 * part, total, 0.0)
-        logits = term if logits is None else logits + term
-    logits = jnp.sum(logits, axis=1, keepdims=True)
-    target = column(labels[...], own, lax.axis_index("x") * own)
-    grad = loss_scale * (1.0 / (1.0 + jnp.exp(-logits)) - target)
-    for x in range(cols):
-        back = (grad * jnp.where(lane == 2 * part, 1.0, sums[x])).astype(bf16)
-        for p in range(peers):
-            send[p * cols + x] = back
-
-
-def back_kernel(held, came, pick_t, send):
-    sums = dot(pick_t[...], came[...])
-    for z in range(send.shape[0]):
-        full = sums[z * held : (z + 1) * held]
-        send[z] = pack(full, full[:, 64:65]).astype(bf16)
+    got = dot(pick[...], table)
+    half = got.shape[0] // 2
+    both = jnp.where(iota((half, LANES), 1) < 64, got[:half], roll(got[half:], 64))
+    blocks = got.shape[0] // LANES
+    lines = [turn(got[b * LANES : (b + 1) * LANES, 64:65]) for b in range(blocks)]
+    lines.append(jnp.zeros((send.shape[1] - half - blocks, LANES), f32))
+    block = jnp.concatenate([both] + lines, axis=0).astype(bf16)
+    for y in range(send.shape[0]):
+        send[y] = block
+
+
+def logit_kernel(part, came, send, sums):
+    total = came[0].astype(f32)
+    for y in range(1, came.shape[0]):
+        total = total + came[y].astype(f32)
+    half = sums.shape[0]
+    lines = total[half:]
+    total = total[:half]
+    sums[...] = total
+    lane = iota((half, LANES), 1)
+    product = total * roll(total, -part)
+    left = jnp.sum(jnp.where(lane < part, product, 0.0), axis=1, keepdims=True)
+    right = jnp.sum(jnp.where((lane >= 64) & (lane < 64 + part), product, 0.0), axis=1, keepdims=True)
+    rows = [turn(side[b * LANES : (b + 1) * LANES]) for side in (left, right) for b in range(half // LANES)]
+    rows.append(jnp.zeros((send.shape[1] - len(rows), LANES), f32))
+    rows = jnp.concatenate(rows, axis=0) + lines * (1.0 / send.shape[0])
+    for x in range(send.shape[0]):
+        send[x] = rows
+
+
+def back_kernel(held, came, labels, sums, pick_t, keep, give):
+    logits = came[0]
+    for x in range(1, came.shape[0]):
+        logits = logits + came[x]
+    grad = loss_scale * (1.0 / (1.0 + jnp.exp(-logits)) - labels[...])
+    half = sums.shape[0]
+    blocks = half // LANES
+    lane = iota((half, LANES), 1)
+    cols = [column(grad[b : b + 1], LANES) for b in range(2 * blocks)]
+    left, right = jnp.concatenate(cols[:blocks], axis=0), jnp.concatenate(cols[blocks:], axis=0)
+    scaled = sums[...] * jnp.where(lane < 64, left, right)
+    sides = [
+        jnp.where(lane < 64, value, jnp.where(lane == 64, line, 0.0))
+        for value, line in ((scaled, left), (roll(scaled, 64), right))
+    ]
+    back = dot(pick_t[...], jnp.concatenate(sides, axis=0).astype(bf16))
+    depth = keep.shape[0]
+    for z in range(2 * depth):
+        full = back[z * held : (z + 1) * held]
+        block = pack(full, full[:, 64:65])
+        if z < depth:
+            keep[z] = block
+        else:
+            give[z - depth] = block.astype(bf16)
+
+
+def join_kernel(keep, came, send):
+    send[...] = (keep[...] + came[...].astype(f32)).astype(bf16)
 
 
 def total_kernel(came, send):
@@ -242,50 +277,57 @@
     head_user,
     head_item,
 ):
-    cols, depth, cores = lax.axis_size("x"), lax.axis_size("z"), lax.axis_size("c")
-    peers = lax.axis_size("y") * cores
+    cols, depth, cores, peers = (lax.axis_size(a) for a in ("x", "z", "c", "y"))
     users, items = user_table.shape[0], item_table.shape[0]
     imps, lists = item_row.shape
     part = enter_user.shape[1] // cols
     held = users + items
-    span = depth * held
-    own = imps // cols
+    span = cores * depth * held
+    mass = peers * imps
+    half = mass // 2
+    pair = [(0, 1), (1, 0)]
     shape = jax.ShapeDtypeStruct
     weights = (enter_user, enter_item, leave_user, leave_item) + tuple(
         v[None] for v in (bias_user, bias_item, head_user, head_item)
     )
 
     send, names = call(
-        lambda *refs: parts_kernel(cols, cores, *refs),
+        lambda *refs: parts_kernel(cols, *refs),
         [shape((peers * cols, FRONT, LANES), bf16), shape((FRONT, LANES), bf16)],
         20_000_000, 2_500_000,
-        user_table, user_scale[None], item_table, user_owner.T, user_row[None], item_owner.T, item_row.T, *weights, fetch=True,
+        user_table, user_scale[None], item_table, user_owner.T, user_row[None], item_owner.T, item_row.T, labels[None],
+        *weights, fetch=True,
     )
     came = swap(send, BLOCK)
-    send = call(
-        lambda *refs: share_kernel(cols, cores, *refs), shape((depth, FRONT, LANES), bf16), 100_000, 200_000, came
-    )
+    send = call(lambda *refs: share_kernel(cols, *refs), shape((depth, FRONT, LANES), bf16), 100_000, 200_000, came)
     table = swap(send, "z")
-    pick, pick_t = call(
+    pick, pick_t, targets = call(
         lambda *refs: pick_kernel(cols, cores, depth, users, held, lists, *refs),
-        [shape((peers * imps, span), bf16), shape((span, peers * imps), bf16)],
+        [shape((mass, span), bf16), shape((span, mass), bf16), shape((8, LANES), f32)],
         100_000_000, 10_000_000,
         came, names,
     )
+    table, pick, pick_t, targets = lax.optimization_barrier((table, pick, pick_t, targets))
+    other = lax.ppermute(table, "c", pair)
     send = call(
-        lambda *refs: fetch_kernel(held, *refs), shape((peers * imps, LANES), bf16), 200_000_000, 1_500_000, table, pick
-    )
-    came = swap(send.reshape(peers * cols, own, LANES), BLOCK)
+        lambda *refs: fetch_kernel(held, *refs),
+        shape((peers, half + 8, LANES), bf16), 200_000_000, 1_500_000,
+        table, other, pick,
+    )
+    came = swap(send, "y")
+    send, sums = call(
+        lambda *refs: logit_kernel(part, *refs),
+        [shape((cols, 8, LANES), f32), shape((half, LANES), f32)], 1_000_000, 500_000,
+        came,
+    )
+    came = swap(send, "x")
+    keep, give = call(
+        lambda *refs: back_kernel(held, *refs),
+        [shape((depth, FRONT, LANES), f32), shape((depth, FRONT, LANES), bf16)], 200_000_000, 1_500_000,
+        came, targets, sums, pick_t,
+    )
     send = call(
-        lambda *refs: loss_kernel(cols, part, *refs),
-        shape((peers * cols, own, LANES), bf16), 1_000_000, 500_000,
-        came, labels[None],
-    )
-    came = swap(send, BLOCK)
-    send = call(
-        lambda *refs: back_kernel(held, *refs),
-        shape((depth, FRONT, LANES), bf16), 200_000_000, 1_500_000,
-        came.reshape(peers * imps, LANES), pick_t,
+        join_kernel, shape((depth, FRONT, LANES), bf16), 100_000, 400_000, keep, lax.ppermute(give, "c", pair)
     )
     came = swap(send, "z")
     send = call(total_kernel, shape((cols, FRONT, LANES), bf16), 100_000, 200_000, came)

time: 102 us -> 100 us (0.980)
  the two profiles are of different devices: /device:TPU:1 before, /device:TPU:32 now
where the time goes in v2:
time: 100 us
  blocking collectives  58.4 us (58%)
  starting transfers between devices  19 us (19%)
  Pallas kernels  11.6 us (12%)
  waiting for transfers between devices  9.46 us (9%)
    all_to_all x5, blocking collectives, swap(): return lax.all_to_all(value, axes, split_axis=0, concat_axis=0, tiled=True)  58.4 us
    all_to_all x1, starting transfers between devices, swap(): return lax.all_to_all(value, axes, split_axis=0, concat_axis=0, tiled=True)  15.2 us
    pallas_call x8, Pallas kernels, call(): pl.pallas_call(kernel, out_shape=outs, in_specs=[spec] * len(args), out_s...  8.42 us
    all_to_all x1, waiting for transfers between devices, swap(): return lax.all_to_all(value, axes, split_axis=0, concat_axis=0, tiled=True)  6.92 us
    pallas_call x1, Pallas kernels, call(): pl.pallas_call(kernel, out_shape=outs, grid=(1,), in_specs=[pl.BlockSpec(...  3.17 us
  transfers between devices with their start and end apart: 3, of which 3 were waited for; matrix products, arithmetic and copies ran while one was open for 0% of the time, Pallas kernels for 4%

profile of v2, /device:TPU:32, one launch (start us, length us, event | category | flops | bytes accessed | tf_op | source)
XLA Modules:
  0.0 100.0 jit_solution(7272766505033524376)
XLA Ops:
  0.6 3.2 %shard_map.167 = (bf16[16,24,128]{2,1,0:T(8,128)(2,1)}, bf16[24,128]{1,0:T(8,128)(2,1)}) custom-call(bf16[8,4096]{1,0:T(8,128)(2,1)} %refs_0_.1, bf16[1,8]{1,0:T(2,128)(2,1)} %bitcast.20, bf16[32,256]{1,0:T(8,128)(2,1)} %refs_2_.2, s32[1,128]{1,0:T(1,128)} %bitcast.21, s32[1,128]{1,0:T(1,128)} %bitcast.22, s32[4,128]{1,0:T(4,128)} %bitcast.18, ...), custom_call_target="tpu_custom_call" | custom-call | flops 20000000 | bytes 2500000 | tf_op jit(solution)/shard_map/pallas_call | solution.py:239
  3.8 14.8 %all_to_all.30.refs_0_ = bf16[16,24,128]{2,1,0:T(8,128)(2,1)S(1)} all-to-all(bf16[16,24,128]{2,1,0:T(8,128)(2,1)} %get-tuple-element.15), channel_id=1, replica_groups=mesh['y'=4,'z'=16,'c'=2,'x'=4] {'y','x'}, dimensions={0} | all-to-all | bytes 196608 | tf_op jit(solution)/shard_map/all_to_all | solution.py:259
  18.7 0.7 shard_map.168
  19.3 15.2 %all-to-all-start.1 = ((bf16[16,24,128]{2,1,0:T(8,128)(2,1)}), bf16[16,24,128]{2,1,0:T(8,128)(2,1)S(1)}, u32[]{:S(2)}, u32[]{:S(2)}) async-start(bf16[16,24,128]{2,1,0:T(8,128)(2,1)} %shard_map.168), calls=%async_computation.1 | async-start | bytes 196608 | tf_op jit(solution)/shard_map/all_to_all | solution.py:259
  34.5 0.7 copy-done.8
  35.2 4.3 %shard_map.169 = (bf16[512,1280]{1,0:T(8,128)(2,1)S(1)}, bf16[1280,512]{1,0:T(8,128)(2,1)S(1)}, f32[8,128]{1,0:T(8,128)S(1)}) custom-call(bf16[16,24,128]{2,1,0:T(8,128)(2,1)S(1)} %all_to_all.30.refs_0_, bf16[24,128]{1,0:T(8,128)(2,1)S(1)} %copy-done.8), custom_call_target="tpu_custom_call" | custom-call | flops 100000000 | bytes 10000000 | tf_op jit(solution)/shard_map/pallas_call | solution.py:248
  39.5 6.9 %all-to-all-done.1.refs_0_ = bf16[16,24,128]{2,1,0:T(8,128)(2,1)S(1)} async-done(((bf16[16,24,128]{2,1,0:T(8,128)(2,1)}), bf16[16,24,128]{2,1,0:T(8,128)(2,1)S(1)}, u32[]{:S(2)}, u32[]{:S(2)}) %all-to-all-start.1) | async-done | bytes 98336 | tf_op jit(solution)/shard_map/all_to_all | solution.py:259
  46.4 1.9 %collective-permute-start = (bf16[16,24,128]{2,1,0:T(8,128)(2,1)S(1)}, bf16[16,24,128]{2,1,0:T(8,128)(2,1)S(1)}, u32[]{:S(2)}, u32[]{:S(2)}) collective-permute-start(bf16[16,24,128]{2,1,0:T(8,128)(2,1)S(1)} %all-to-all-done.1.refs_0_), channel_id=1, source_target_pairs={{0,4},{4,0},{1,5},{5,1},{2,6},{6,2},{3,7},{7,3},{8,12},{12,8},{9,1... | collective-permute-start | bytes 294920 | tf_op jit(solution)/shard_map/ppermute | solution.py:311
  48.3 1.3 %collective-permute-done.refs_1_ = bf16[16,24,128]{2,1,0:T(8,128)(2,1)S(1)} collective-permute-done((bf16[16,24,128]{2,1,0:T(8,128)(2,1)S(1)}, bf16[16,24,128]{2,1,0:T(8,128)(2,1)S(1)}, u32[]{:S(2)}, u32[]{:S(2)}) %collective-permute-start) | collective-permute-done | bytes 98336 | tf_op jit(solution)/shard_map/ppermute | solution.py:311
  49.6 1.0 %shard_map.170 = bf16[4,264,128]{2,1,0:T(8,128)(2,1)S(1)} custom-call(bf16[16,24,128]{2,1,0:T(8,128)(2,1)S(1)} %all-to-all-done.1.refs_0_, bf16[16,24,128]{2,1,0:T(8,128)(2,1)S(1)} %collective-permute-done.refs_1_, bf16[512,1280]{1,0:T(8,128)(2,1)S(1)} %get-tuple-element.21.refs_2_), custom_call_target="tpu_custom_call" | custom-call | flops 200000000 | bytes 1500000 | tf_op jit(solution)/shard_map/pallas_call | solution.py:248
  50.6 9.7 %all_to_all.31.refs_0_ = bf16[4,264,128]{2,1,0:T(8,128)(2,1)S(1)} all-to-all(bf16[4,264,128]{2,1,0:T(8,128)(2,1)S(1)} %shard_map.170), channel_id=1, replica_groups=mesh['y'=4,'z'=16,'c'=2,'x'=4] {'y'}, dimensions={0} | all-to-all | bytes 540672 | tf_op jit(solution)/shard_map/all_to_all | solution.py:259
  60.4 0.0 copy-start.4
  60.4 0.0 copy-start.5
  60.4 0.0 copy-start.6
  60.4 0.0 copy-start.7
  60.4 0.2 shard_map.171
  60.7 7.8 %all_to_all.32.refs_0_ = f32[4,8,128]{2,1,0:T(8,128)S(1)} all-to-all(f32[4,8,128]{2,1,0:T(8,128)S(1)} %get-tuple-element.22), channel_id=1, replica_groups=mesh['y'=4,'z'=16,'c'=2,'x'=4] {'x'}, dimensions={0} | all-to-all | bytes 32768 | tf_op jit(solution)/shard_map/all_to_all | solution.py:259
  68.5 0.9 shard_map.172
  69.4 1.9 %collective-permute-start.1 = (bf16[16,24,128]{2,1,0:T(8,128)(2,1)S(1)}, bf16[16,24,128]{2,1,0:T(8,128)(2,1)S(1)}, u32[]{:S(2)}, u32[]{:S(2)}) collective-permute-start(bf16[16,24,128]{2,1,0:T(8,128)(2,1)S(1)} %get-tuple-element.27), channel_id=1, source_target_pairs={{0,4},{4,0},{1,5},{5,1},{2,6},{6,2},{3,7},{7,3},{8,12},{12,8},{9,1... | collective-permute-start | bytes 294920 | tf_op jit(solution)/shard_map/ppermute | solution.py:330
  71.3 1.3 %collective-permute-done.1.came = bf16[16,24,128]{2,1,0:T(8,128)(2,1)S(1)} collective-permute-done((bf16[16,24,128]{2,1,0:T(8,128)(2,1)S(1)}, bf16[16,24,128]{2,1,0:T(8,128)(2,1)S(1)}, u32[]{:S(2)}, u32[]{:S(2)}) %collective-permute-start.1) | collective-permute-done | bytes 98336 | tf_op jit(solution)/shard_map/ppermute | solution.py:330
  72.6 18.2 %all_to_all.33.came = bf16[16,24,128]{2,1,0:T(8,128)(2,1)S(1)} all-to-all(bf16[16,24,128]{2,1,0:T(8,128)(2,1)S(1)} %shard_map.173), channel_id=1, replica_groups=mesh['y'=4,'z'=16,'c'=2,'x'=4] {'z'}, dimensions={0} | all-to-all | bytes 196608 | tf_op jit(solution)/shard_map/all_to_all | solution.py:259
  90.8 7.8 %all_to_all.34.refs_0_ = bf16[4,24,128]{2,1,0:T(8,128)(2,1)S(1)} all-to-all(bf16[4,24,128]{2,1,0:T(8,128)(2,1)S(1)} %shard_map.174), channel_id=1, replica_groups=mesh['y'=4,'z'=16,'c'=2,'x'=4] {'x'}, dimensions={0} | all-to-all | bytes 49152 | tf_op jit(solution)/shard_map/all_to_all | solution.py:259
  98.6 0.0 copy-done.1
  98.6 1.3 %shard_map.175 = (f32[8,4096]{1,0:T(8,128)}, f32[32,256]{1,0:T(8,128)}) custom-call(bf16[4,24,128]{2,1,0:T(8,128)(2,1)S(1)} %all_to_all.34.refs_0_, bf16[4096,128]{1,0:T(8,128)(2,1)S(1)} %copy-done, bf16[256,128]{1,0:T(8,128)(2,1)S(1)} %copy-done.2, bf16[128,4096]{1,0:T(8,128)(2,1)S(1)} %copy-done.1, bf16[128,256]{1,0:T(8,128)(2,1)S(1)} %copy-done.3, ...), custom_call_target="tpu_custom_call" | custom-call | flops 20000000 | bytes 2500000 | tf_op jit(solution)/shard_map/pallas_call | solution.py:248
  (14 shorter events, 0.1 us)
Async XLA Ops:
  19.3 27.1 %all-to-all-start.1 = ((bf16[16,24,128]{2,1,0:T(8,128)(2,1)}), bf16[16,24,128]{2,1,0:T(8,128)(2,1)S(1)}, u32[]{:S(2)}, u32[]{:S(2)}) async-start(bf16[16,24,128]{2,1,0:T(8,128)(2,1)} %shard_map.168), calls=%async_computation.1 | async-start | bytes 196608 | tf_op jit(solution)/shard_map/all_to_all | solution.py:259
  34.5 0.7 copy-start.8
  46.4 3.2 %collective-permute-start = (bf16[16,24,128]{2,1,0:T(8,128)(2,1)S(1)}, bf16[16,24,128]{2,1,0:T(8,128)(2,1)S(1)}, u32[]{:S(2)}, u32[]{:S(2)}) collective-permute-start(bf16[16,24,128]{2,1,0:T(8,128)(2,1)S(1)} %all-to-all-done.1.refs_0_), channel_id=1, source_target_pairs={{0,4},{4,0},{1,5},{5,1},{2,6},{6,2},{3,7},{7,3},{8,12},{12,8},{9,1... | collective-permute-start | bytes 294920 | tf_op jit(solution)/shard_map/ppermute | solution.py:311
  60.4 38.2 %copy-start = (bf16[4096,128]{1,0:T(8,128)(2,1)S(1)}, bf16[4096,128]{1,0:T(8,128)(2,1)}, u32[]{:S(2)}) copy-start(bf16[4096,128]{1,0:T(8,128)(2,1)} %refs_1_.1) | copy-start | bytes 3145732
  60.4 38.2 %copy-start.1 = (bf16[128,4096]{1,0:T(8,128)(2,1)S(1)}, bf16[128,4096]{1,0:T(8,128)(2,1)}, u32[]{:S(2)}) copy-start(bf16[128,4096]{1,0:T(8,128)(2,1)} %refs_3_.1) | copy-start | bytes 3145732
  60.4 38.2 %copy-start.2 = (bf16[256,128]{1,0:T(8,128)(2,1)S(1)}, bf16[256,128]{1,0:T(8,128)(2,1)}, u32[]{:S(2)}) copy-start(bf16[256,128]{1,0:T(8,128)(2,1)} %refs_2_.3) | copy-start | bytes 196612
  60.4 38.2 %copy-start.3 = (bf16[128,256]{1,0:T(8,128)(2,1)S(1)}, bf16[128,256]{1,0:T(8,128)(2,1)}, u32[]{:S(2)}) copy-start(bf16[128,256]{1,0:T(8,128)(2,1)} %refs_4_.1) | copy-start | bytes 196612
  60.4 38.2 %copy-start.4 = (f32[4096]{0:T(1024)S(1)}, f32[4096]{0:T(1024)}, u32[]{:S(2)}) copy-start(f32[4096]{0:T(1024)} %param.28) | copy-start | bytes 49156
  60.4 38.2 %copy-start.5 = (f32[4096]{0:T(1024)S(1)}, f32[4096]{0:T(1024)}, u32[]{:S(2)}) copy-start(f32[4096]{0:T(1024)} %param.30) | copy-start | bytes 49156
  60.4 38.2 %copy-start.6 = (f32[256]{0:T(256)S(1)}, f32[256]{0:T(256)}, u32[]{:S(2)}) copy-start(f32[256]{0:T(256)} %param.29) | copy-start | bytes 3076
  60.4 38.2 %copy-start.7 = (f32[256]{0:T(256)S(1)}, f32[256]{0:T(256)}, u32[]{:S(2)}) copy-start(f32[256]{0:T(256)} %param.31) | copy-start | bytes 3076
  69.4 3.2 %collective-permute-start.1 = (bf16[16,24,128]{2,1,0:T(8,128)(2,1)S(1)}, bf16[16,24,128]{2,1,0:T(8,128)(2,1)S(1)}, u32[]{:S(2)}, u32[]{:S(2)}) collective-permute-start(bf16[16,24,128]{2,1,0:T(8,128)(2,1)S(1)} %get-tuple-element.27), channel_id=1, source_target_pairs={{0,4},{4,0},{1,5},{5,1},{2,6},{6,2},{3,7},{7,3},{8,12},{12,8},{9,1... | collective-permute-start | bytes 294920 | tf_op jit(solution)/shard_map/ppermute | solution.py:330

commit v3 on v1

v3 whole, which is shorter than its diff:
```python
import jax
import jax.numpy as jnp
from jax import lax
from jax.experimental import pallas as pl
from jax.experimental.pallas import tpu as pltpu
from jax.sharding import Mesh, PartitionSpec as P

loss_scale = 128.0
bf16 = jnp.bfloat16
f32 = jnp.float32
i32 = jnp.int32
EMB = ("y", "z", "c")
BLOCK = ("y", "c", "x")
LANES = 128
TILES = 3
SLOTS = 4


def dot(a, b, ca=1, cb=0):
    return lax.dot_general(a, b, (((ca,), (cb,)), ((), ())), preferred_element_type=f32)


def iota(shape, axis):
    return lax.broadcasted_iota(i32, shape, axis)


def roll(value, shift):
    shift = shift % LANES
    return pltpu.roll(value, shift, 1) if shift else value


def column(row, rows, first=0):
    wide = (rows, row.shape[1])
    hit = iota(wide, 1) == iota(wide, 0) + first
    return jnp.sum(jnp.where(hit, row, 0.0), axis=1, keepdims=True)


def row_parts(rows, enter, leave, bias, head):
    wide = rows.astype(f32)
    low = dot(rows, enter)
    carry = dot((wide * head).astype(bf16), leave, 1, 1)
    return low, carry, jnp.sum(head * (wide * bias + wide), axis=1, keepdims=True)


def split(value):
    return [value[8 * t : 8 * t + 8] for t in range(TILES)]


def unit(value, octet):
    if value == 8:
        return (octet * SLOTS + 2, 2) if octet < 4 else (3, 2)
    q = octet + 5 * (value // 4)
    return (value % 4) * SLOTS + q % SLOTS, q // SLOTS


def exchange(blocks):
    group = iota((8, LANES), 1) // 8
    for bit in (1, 2, 4, 8):
        low = (group & bit) == 0
        after = list(blocks)
        for z in range(16):
            if z & bit == 0:
                a, b = blocks[z], blocks[z | bit]
                after[z] = [jnp.where(low, a[t], roll(b[t], 8 * bit)) for t in range(TILES)]
                after[z | bit] = [jnp.where(low, roll(a[t], -8 * bit), b[t]) for t in range(TILES)]
        blocks = after
    return blocks


def parts_kernel(
    table_u, scale, table_i, owner_u, row_u, owner_i, row_i, labels, enter_u, enter_i, leave_u, leave_i,
    bias_u, bias_i, head_u, head_i, send,
):
    users = table_u.shape[0]
    scales = column(scale[...].astype(f32), users)
    rows = (table_u[...].astype(f32) * scales).astype(bf16)
    low_u, carry_u, line_u = row_parts(rows, enter_u[...], leave_u[...], bias_u[...], head_u[...])
    low_i, carry_i, line_i = row_parts(table_i[...], enter_i[...], leave_i[...], bias_i[...], head_i[...])
    octets = [low_u] + [low_i[8 * o : 8 * o + 8] for o in range(4)]
    octets += [carry_u] + [carry_i[8 * o : 8 * o + 8] for o in range(4)]
    lines = [line_u] + [line_i[8 * o : 8 * o + 8] for o in range(4)]
    lane = iota((8, LANES), 1)
    octets = [roll(v, q) for q, v in enumerate(octets)]
    flat = jnp.zeros((8, LANES), f32)
    for o, line in enumerate(lines):
        flat = jnp.where(lane == (32 * o + 10 if o < 4 else 11), line, flat)
    parts = [v[...].astype(f32) for v in (owner_u, row_u, owner_i, row_i)]
    rest = labels[...]
    for _ in range(3):
        piece = rest.astype(bf16).astype(f32)
        parts.append(piece)
        rest = rest - piece
    names = jnp.concatenate(parts + [jnp.zeros((3, LANES), f32)], axis=0)
    mine = lax.axis_index("x")
    share = names[0:4]
    for x in range(1, 4):
        share = jnp.where(mine == x, names[4 * x : 4 * x + 4], share)
    moved = roll(share, 16)
    share = jnp.concatenate([v[r : r + 1] for r in range(4) for v in (moved, share)], axis=0)
    flat = jnp.where(lane % 32 < 16, flat, share)
    for p in range(send.shape[0]):
        at = (lane - p) & 31
        tile = jnp.zeros((8, LANES), f32)
        for q, value in enumerate(octets):
            tile = jnp.where(at == q, value, tile)
        send[p] = (roll(tile, -p) + flat).astype(bf16)


def share_kernel(came, send):
    lane = iota((8, LANES), 1)
    planes = []
    for b in range(came.shape[0] // 4):
        total = came[4 * b].astype(f32)
        for x in range(1, 4):
            total = total + came[4 * b + x].astype(f32)
        planes.append(roll(total, b))
    tiles = []
    for t in range(TILES):
        tile = jnp.zeros((8, LANES), f32)
        for sub in range(SLOTS):
            q = SLOTS * t + sub
            at = (lane - q) & 31
            value = jnp.zeros((8, LANES), f32)
            for b, plane in enumerate(planes):
                value = jnp.where(at == b, plane, value)
            tile = tile + roll(value, 8 * sub - q)
        tiles.append(tile)
    block = jnp.concatenate(tiles, axis=0).astype(bf16)
    for z in range(send.shape[0]):
        send[z] = block


def pick_kernel(came, owners, rows, labels):
    blocks = came.shape[0] // 4
    names, targets = [], []
    odd = iota((8, LANES), 0) % 2 == 1
    side = iota((1, LANES), 1) % 32 >= 16
    for b in range(blocks):
        share = [came[4 * b + x].astype(f32) for x in range(4)]
        share = jnp.concatenate([jnp.where(odd, v, roll(v, -16)) for v in share], axis=0)
        block = jnp.concatenate([jnp.where(side, share[r + 1 : r + 2], share[r : r + 1]) for r in range(0, 32, 2)], axis=0)
        names.append(block.astype(i32))
        targets.append((block[10:11] + block[11:12]) + block[12:13])
    labels[...] = jnp.concatenate(targets, axis=0)
    names = jnp.concatenate(names, axis=1)
    mass = names.shape[1]
    ids = iota((LANES, mass), 0)
    tall = iota((32, mass), 0)
    for j in range(5):
        owner = names[j + 1 : j + 2] if j else names[0:1]
        row = names[j + 5 : j + 6] if j else names[1:2]
        y, z, c = owner // 32, (owner // 2) % 16, owner % 2
        owners[j] = jnp.where(ids == z * 8 + y * 2 + c, 1.0, 0.0).astype(bf16)
        if j:
            rows[32 * j - 24 : 32 * j + 8, :] = jnp.where(tall == row, 1.0, 0.0)
        else:
            rows[0:8, :] = jnp.where(tall[:8] == row, 1.0, 0.0)


def fetch_kernel(came, owners, rows, send, sums):
    blocks = exchange([split(came[z].astype(f32)) for z in range(came.shape[0])])

    def table(octets):
        tiles = []
        for w in range(9):
            for o in octets:
                g, t = unit(w, o)
                tiles.append(blocks[g][t])
        return jnp.concatenate(tiles, axis=0).astype(bf16)

    got = dot(table([0]), owners[0])
    mask = rows[0:8, :]
    total = [got[8 * w : 8 * w + 8] * mask for w in range(9)]
    listed = table([1, 2, 3, 4])
    for j in range(1, 5):
        got = dot(listed, owners[j])
        masks = [rows[32 * j - 24 + 8 * o : 32 * j - 16 + 8 * o, :] for o in range(4)]
        for w in range(9):
            for o in range(4):
                at = 8 * (4 * w + o)
                total[w] = total[w] + got[at : at + 8] * masks[o]
    total = [jnp.sum(v, axis=0, keepdims=True) for v in total]
    logits = total[8] * (1.0 / send.shape[0])
    for w in range(4):
        logits = logits + total[w] * total[w + 4]
    sums[...] = jnp.concatenate(total + [jnp.zeros((7, logits.shape[1]), f32)], axis=0)
    logits = jnp.concatenate([logits[:, LANES * b : LANES * (b + 1)] for b in range(8)], axis=0)
    for p in range(send.shape[0]):
        send[p] = logits


def back_kernel(came, labels, sums, owners, rows, send):
    logits = came[0]
    for p in range(1, came.shape[0]):
        logits = logits + came[p]
    grad = loss_scale * (1.0 / (1.0 + jnp.exp(-logits)) - labels[...])
    grad = jnp.concatenate([grad[b : b + 1] for b in range(8)], axis=1)
    back = [grad * sums[w : w + 1, :] for w in range(8)] + [grad]

    def scatter(j, masks):
        tall = jnp.concatenate([mask * value for value in back for mask in masks], axis=0)
        return dot(tall.astype(bf16), owners[j], 1, 1)

    own = scatter(0, [rows[0:8, :]])
    listed = None
    for j in range(1, 5):
        part = scatter(j, [rows[32 * j - 24 + 8 * o : 32 * j - 16 + 8 * o, :] for o in range(4)])
        listed = part if listed is None else listed + part
    empty = jnp.zeros((8, LANES), f32)
    blocks = [[empty] * TILES for _ in range(16)]
    for w in range(9):
        for o in range(5):
            g, t = unit(w, o)
            at = 8 * (4 * w + o - 1)
            blocks[g][t] = listed[at : at + 8] if o else own[8 * w : 8 * w + 8]
    blocks = exchange(blocks)
    for z in range(send.shape[0]):
        send[z] = jnp.concatenate(blocks[z], axis=0).astype(bf16)


def total_kernel(came, send):
    lane = iota((8, LANES), 1)
    total = came[0].astype(f32)
    for z in range(1, came.shape[0]):
        total = total + came[z].astype(f32)
    tiles = split(total)
    values = [roll(tiles[q // SLOTS], q - 8 * (q % SLOTS)) for q in range(SLOTS * TILES)]
    for b in range(send.shape[0] // 4):
        at = (lane - b) & 31
        tile = jnp.zeros((8, LANES), f32)
        for q, value in enumerate(values):
            tile = jnp.where(at == q, value, tile)
        tile = roll(tile, -b).astype(bf16)
        for x in range(4):
            send[4 * b + x] = tile


def grad_kernel(users, came, enter_u, enter_i, leave_u, leave_i, bias_u, bias_i, head_u, head_i, out_u, out_i):
    lane = iota((8, LANES), 1)
    ranks = [jnp.zeros((8, LANES), f32)] * 10
    ats = [(lane - q) & 31 for q in range(10)]
    for p in range(came.shape[0]):
        tile = came[p].astype(f32)
        if p == 0:
            hits = [lane == (32 * o + 10 if o < 4 else 11) for o in range(5)]
            lines = [jnp.sum(jnp.where(hit, tile, 0.0), axis=1, keepdims=True) for hit in hits]
        tile = roll(tile, p)
        for q in range(10):
            ranks[q] = jnp.where(ats[q] == p, tile, ranks[q])
    ranks = [roll(v, -q) for q, v in enumerate(ranks)]
    low = jnp.concatenate(ranks[:5], axis=0)
    carry = jnp.concatenate(ranks[5:], axis=0)
    line = jnp.concatenate(lines, axis=0)
    held = low.shape[0]
    for out, a, b, enter, leave, bias, head in (
        (out_u, 0, users, enter_u, leave_u, bias_u, head_u),
        (out_i, users, held, enter_i, leave_i, bias_i, head_i),
    ):
        hidden = dot(low[a:b].astype(bf16), leave[...])
        back = dot(carry[a:b].astype(bf16), enter[...], 1, 1)
        out[...] = head[...] * (hidden + line[a:b] * (bias[...] + 1.0)) + back


def call(kernel, outs, flops, bytes_accessed, *args, fetch=False):
    many = isinstance(outs, list)
    spec = pl.BlockSpec(memory_space=pltpu.VMEM)
    if fetch:
        return pl.pallas_call(
            kernel,
            out_shape=outs,
            grid=(1,),
            in_specs=[pl.BlockSpec(a.shape, lambda i: (0, 0)) for a in args],
            out_specs=[spec] * len(outs) if many else spec,
            compiler_params=pltpu.CompilerParams(vmem_limit_bytes=60 * 1024 * 1024),
            cost_estimate=pl.CostEstimate(flops=flops, bytes_accessed=bytes_accessed, transcendentals=0),
        )(*args)
    return pl.pallas_call(
        kernel,
        out_shape=outs,
        in_specs=[spec] * len(args),
        out_specs=[spec] * len(outs) if many else spec,
        compiler_params=pltpu.CompilerParams(vmem_limit_bytes=40 * 1024 * 1024),
        cost_estimate=pl.CostEstimate(flops=flops, bytes_accessed=bytes_accessed, transcendentals=0),
    )(*args)


def swap(value, axes):
    return lax.all_to_all(value, axes, split_axis=0, concat_axis=0, tiled=True)


def body(
    user_table,
    user_scale,
    item_table,
    user_owner,
    user_row,
    item_owner,
    item_row,
    labels,
    enter_user,
    enter_item,
    leave_user,
    leave_item,
    bias_user,
    bias_item,
    head_user,
    head_item,
):
    depth = lax.axis_size("z")
    plane = lax.axis_size("y") * lax.axis_size("c") * lax.axis_size("x")
    users = user_table.shape[0]
    mass = labels.shape[0] * lax.axis_size("y") * lax.axis_size("c")
    block = 8 * TILES
    shape = jax.ShapeDtypeStruct
    weights = (enter_user, enter_item, leave_user, leave_item) + tuple(
        v[None] for v in (bias_user, bias_item, head_user, head_item)
    )

    send = call(
        parts_kernel, shape((plane, 8, LANES), bf16), 20_000_000, 2_500_000,
        user_table, user_scale[None], item_table, user_owner.T, user_row[None], item_owner.T, item_row.T, labels[None],
        *weights, fetch=True,
    )
    came = swap(send, BLOCK)
    send = call(share_kernel, shape((depth, block, LANES), bf16), 100_000, 200_000, came)
    table = swap(send, "z")
    owners, rows, targets = call(
        pick_kernel,
        [shape((5, LANES, mass), bf16), shape((136, mass), f32), shape((8, LANES), f32)],
        10_000_000, 3_000_000,
        came,
    )
    send, sums = call(
        fetch_kernel, [shape((plane, 8, LANES), f32), shape((16, mass), f32)], 400_000_000, 3_000_000,
        table, owners, rows,
    )
    came = swap(send, BLOCK)
    send = call(
        back_kernel, shape((depth, block, LANES), bf16), 400_000_000, 3_000_000, came, targets, sums, owners, rows
    )
    came = swap(send, "z")
    send = call(total_kernel, shape((plane, 8, LANES), bf16), 100_000, 200_000, came)
    came = swap(send, BLOCK)
    user_grad, item_grad = call(
        lambda *refs: grad_kernel(users, *refs),
        [shape(user_table.shape, f32), shape(item_table.shape, f32)],
        20_000_000, 2_500_000,
        came, *weights,
    )
    return (user_grad, item_grad)


def solution(mesh):
    cols = mesh.shape["col"]
    cells = mesh.devices.reshape(-1, 16, 2, cols)
    fine = Mesh(cells, ("y", "z", "c", "x"))
    return jax.shard_map(
        body,
        mesh=fine,
        in_specs=(
            P(EMB, "x"),
            P(EMB),
            P(EMB, "x"),
            P(EMB, None),
            P(EMB),
            P(EMB, None),
            P(EMB, None),
            P(EMB),
            P("x", None),
            P("x", None),
            P(None, "x"),
            P(None, "x"),
            P("x"),
            P("x"),
            P("x"),
            P("x"),
        ),
        out_specs=(P(EMB, "x"), P(EMB, "x")),
        check_vma=False,
    )
```

time: 102 us -> 92.6 us (0.908); the launches traced: 100 us -> 92.3 us
  blocking collectives: 67.7 us -> 58.6 us
  waiting for transfers between devices: 7.35 us -> 11.3 us
  Pallas kernels: 10.5 us -> 8.54 us
    all_to_all x5 -> x4, blocking collectives: 67.7 us -> 58.6 us  [swap(): return lax.all_to_all(value, axes, split_axis=0, concat_axis=0, tiled=True)]
    all_to_all x1, waiting for transfers between devices: 7.35 us -> 11.3 us  [swap(): return lax.all_to_all(value, axes, split_axis=0, concat_axis=0, tiled=True)]
    pallas_call x7 -> x6, Pallas kernels: 7.42 us -> 5.34 us  [call(): pl.pallas_call(kernel, out_shape=outs, in_specs=[spec] * len(args), out_s...]
  transfers between devices with their start and end apart: 1 -> 1, of which waited for: 1 -> 1; matrix products, arithmetic and copies ran while one was open for 0% -> 0% of each run, Pallas kernels for 4% -> 1%
where the time goes in v3:
time: 92.6 us; the launch traced here: 92.3 us
  blocking collectives  58.6 us (63%)
  starting transfers between devices  13 us (14%)
  waiting for transfers between devices  11.3 us (12%)
  Pallas kernels  8.54 us (9%)
    all_to_all x4, blocking collectives, swap(): return lax.all_to_all(value, axes, split_axis=0, concat_axis=0, tiled=True)  58.6 us
    all_to_all x1, starting transfers between devices, swap(): return lax.all_to_all(value, axes, split_axis=0, concat_axis=0, tiled=True)  13 us
    all_to_all x1, waiting for transfers between devices, swap(): return lax.all_to_all(value, axes, split_axis=0, concat_axis=0, tiled=True)  11.3 us
    pallas_call x6, Pallas kernels, call(): pl.pallas_call(kernel, out_shape=outs, in_specs=[spec] * len(args), out_s...  5.34 us
    pallas_call x1, Pallas kernels, call(): pl.pallas_call(kernel, out_shape=outs, grid=(1,), in_specs=[pl.BlockSpec(...  3.21 us
  transfers between devices with their start and end apart: 1, of which 1 were waited for; matrix products, arithmetic and copies ran while one was open for 0% of the time, Pallas kernels for 1%

profile of v3, /device:TPU:1, one launch (start us, length us, event | category | flops | bytes accessed | tf_op | source)
XLA Modules:
  0.0 92.3 jit_solution(10002378850104907199)
XLA Ops:
  0.6 3.2 %shard_map.167 = bf16[32,8,128]{2,1,0:T(8,128)(2,1)} custom-call(bf16[8,4096]{1,0:T(8,128)(2,1)} %table_u.1, bf16[1,8]{1,0:T(2,128)(2,1)} %bitcast.20, bf16[32,256]{1,0:T(8,128)(2,1)} %table_i.1, s32[1,128]{1,0:T(1,128)} %bitcast.21, s32[1,128]{1,0:T(1,128)} %bitcast.22, s32[4,128]{1,0:T(4,128)} %bitcast.18, s32[4,128]{1,0:T(4,128)} %bitcast.19, ...), custom_call_target="tpu_custom_call" | custom-call | flops 20000000 | bytes 2500000 | tf_op jit(solution)/shard_map/pallas_call | solution.py:268
  3.8 17.8 %all_to_all.25.came = bf16[32,8,128]{2,1,0:T(8,128)(2,1)S(1)} all-to-all(bf16[32,8,128]{2,1,0:T(8,128)(2,1)} %shard_map.167), channel_id=1, replica_groups=mesh['y'=4,'z'=16,'c'=2,'x'=4] {'y','c','x'}, dimensions={0} | all-to-all | bytes 131072 | tf_op jit(solution)/shard_map/all_to_all | solution.py:288
  21.6 0.8 shard_map.168
  22.4 13.0 %all-to-all-start.1 = ((bf16[16,24,128]{2,1,0:T(8,128)(2,1)}), bf16[16,24,128]{2,1,0:T(8,128)(2,1)S(1)}, u32[]{:S(2)}, u32[]{:S(2)}) async-start(bf16[16,24,128]{2,1,0:T(8,128)(2,1)} %shard_map.168), calls=%async_computation.1 | async-start | bytes 196608 | tf_op jit(solution)/shard_map/all_to_all | solution.py:288
  35.4 0.6 shard_map.169
  36.0 11.3 %all-to-all-done.1.came = bf16[16,24,128]{2,1,0:T(8,128)(2,1)S(1)} async-done(((bf16[16,24,128]{2,1,0:T(8,128)(2,1)}), bf16[16,24,128]{2,1,0:T(8,128)(2,1)S(1)}, u32[]{:S(2)}, u32[]{:S(2)}) %all-to-all-start.1) | async-done | bytes 98336 | tf_op jit(solution)/shard_map/all_to_all | solution.py:288
  47.3 1.2 %shard_map.170 = (f32[32,8,128]{2,1,0:T(8,128)S(1)}, f32[16,1024]{1,0:T(8,128)S(1)}) custom-call(bf16[16,24,128]{2,1,0:T(8,128)(2,1)S(1)} %all-to-all-done.1.came, bf16[5,128,1024]{2,1,0:T(8,128)(2,1)S(1)} %get-tuple-element.7.owners, f32[136,1024]{1,0:T(8,128)S(1)} %get-tuple-element.8.rows), custom_call_target="tpu_custom_call" | custom-call | flops 400000000 | bytes 3000000 | tf_op jit(solution)/shard_map/pallas_call | solution.py:277
  48.5 13.2 %all_to_all.26.came = f32[32,8,128]{2,1,0:T(8,128)S(1)} all-to-all(f32[32,8,128]{2,1,0:T(8,128)S(1)} %get-tuple-element.9), channel_id=1, replica_groups=mesh['y'=4,'z'=16,'c'=2,'x'=4] {'y','c','x'}, dimensions={0} | all-to-all | bytes 262144 | tf_op jit(solution)/shard_map/all_to_all | solution.py:288
  61.7 0.0 copy-start.4
  61.7 0.0 copy-start.5
  61.8 0.0 copy-start.6
  61.8 0.0 copy-start.7
  61.8 1.2 %shard_map.171 = bf16[16,24,128]{2,1,0:T(8,128)(2,1)S(1)} custom-call(f32[32,8,128]{2,1,0:T(8,128)S(1)} %all_to_all.26.came, f32[8,128]{1,0:T(8,128)S(1)} %get-tuple-element.10.labels, f32[16,1024]{1,0:T(8,128)S(1)} %get-tuple-element.11.sums, bf16[5,128,1024]{2,1,0:T(8,128)(2,1)S(1)} %get-tuple-element.7.owners, f32[136,1024]{1,0:T(8,128)S(1)} %get-tuple-element.8.rows), custom_call_target="tpu_custom_call" | custom-call | flops 400000000 | bytes 3000000 | tf_op jit(solution)/shard_map/pallas_call | solution.py:277
  63.0 14.8 %all_to_all.27.came = bf16[16,24,128]{2,1,0:T(8,128)(2,1)S(1)} all-to-all(bf16[16,24,128]{2,1,0:T(8,128)(2,1)S(1)} %shard_map.171), channel_id=1, replica_groups=mesh['y'=4,'z'=16,'c'=2,'x'=4] {'z'}, dimensions={0} | all-to-all | bytes 196608 | tf_op jit(solution)/shard_map/all_to_all | solution.py:288
  77.8 0.2 shard_map.172
  78.0 12.9 %all_to_all.28.refs_0_ = bf16[32,8,128]{2,1,0:T(8,128)(2,1)S(1)} all-to-all(bf16[32,8,128]{2,1,0:T(8,128)(2,1)S(1)} %shard_map.172), channel_id=1, replica_groups=mesh['y'=4,'z'=16,'c'=2,'x'=4] {'y','c','x'}, dimensions={0} | all-to-all | bytes 131072 | tf_op jit(solution)/shard_map/all_to_all | solution.py:288
  90.8 0.0 copy-done
  90.8 0.0 copy-done.1
  90.8 0.0 copy-done.2
  90.9 0.0 copy-done.3
  90.9 0.0 copy-done.4
  90.9 0.0 copy-done.5
  90.9 0.0 copy-done.6
  90.9 1.4 %shard_map.173 = (f32[8,4096]{1,0:T(8,128)}, f32[32,256]{1,0:T(8,128)}) custom-call(bf16[32,8,128]{2,1,0:T(8,128)(2,1)S(1)} %all_to_all.28.refs_0_, bf16[4096,128]{1,0:T(8,128)(2,1)S(1)} %copy-done, bf16[256,128]{1,0:T(8,128)(2,1)S(1)} %copy-done.2, bf16[128,4096]{1,0:T(8,128)(2,1)S(1)} %copy-done.1, bf16[128,256]{1,0:T(8,128)(2,1)S(1)} %copy-done.3, ...), custom_call_target="tpu_custom_call" | custom-call | flops 20000000 | bytes 2500000 | tf_op jit(solution)/shard_map/pallas_call | solution.py:277
  (5 shorter events, 0.0 us)
Async XLA Ops:
  22.4 24.9 %all-to-all-start.1 = ((bf16[16,24,128]{2,1,0:T(8,128)(2,1)}), bf16[16,24,128]{2,1,0:T(8,128)(2,1)S(1)}, u32[]{:S(2)}, u32[]{:S(2)}) async-start(bf16[16,24,128]{2,1,0:T(8,128)(2,1)} %shard_map.168), calls=%async_computation.1 | async-start | bytes 196608 | tf_op jit(solution)/shard_map/all_to_all | solution.py:288
  61.7 29.1 %copy-start = (bf16[4096,128]{1,0:T(8,128)(2,1)S(1)}, bf16[4096,128]{1,0:T(8,128)(2,1)}, u32[]{:S(2)}) copy-start(bf16[4096,128]{1,0:T(8,128)(2,1)} %refs_1_.1) | copy-start | bytes 3145732
  61.7 29.1 %copy-start.1 = (bf16[128,4096]{1,0:T(8,128)(2,1)S(1)}, bf16[128,4096]{1,0:T(8,128)(2,1)}, u32[]{:S(2)}) copy-start(bf16[128,4096]{1,0:T(8,128)(2,1)} %refs_3_.1) | copy-start | bytes 3145732
  61.7 29.1 %copy-start.2 = (bf16[256,128]{1,0:T(8,128)(2,1)S(1)}, bf16[256,128]{1,0:T(8,128)(2,1)}, u32[]{:S(2)}) copy-start(bf16[256,128]{1,0:T(8,128)(2,1)} %refs_2_.1) | copy-start | bytes 196612
  61.7 29.1 %copy-start.3 = (bf16[128,256]{1,0:T(8,128)(2,1)S(1)}, bf16[128,256]{1,0:T(8,128)(2,1)}, u32[]{:S(2)}) copy-start(bf16[128,256]{1,0:T(8,128)(2,1)} %refs_4_.1) | copy-start | bytes 196612
  61.7 29.1 %copy-start.4 = (f32[4096]{0:T(1024)S(1)}, f32[4096]{0:T(1024)}, u32[]{:S(2)}) copy-start(f32[4096]{0:T(1024)} %param.28) | copy-start | bytes 49156
  61.7 29.1 %copy-start.5 = (f32[4096]{0:T(1024)S(1)}, f32[4096]{0:T(1024)}, u32[]{:S(2)}) copy-start(f32[4096]{0:T(1024)} %param.30) | copy-start | bytes 49156
  61.8 29.1 %copy-start.6 = (f32[256]{0:T(256)S(1)}, f32[256]{0:T(256)}, u32[]{:S(2)}) copy-start(f32[256]{0:T(256)} %param.29) | copy-start | bytes 3076
  61.8 29.1 %copy-start.7 = (f32[256]{0:T(256)S(1)}, f32[256]{0:T(256)}, u32[]{:S(2)}) copy-start(f32[256]{0:T(256)} %param.31) | copy-start | bytes 3076

commit v4 on v3

--- a/solution.py
+++ b/solution.py
@@ -145,15 +145,19 @@
     names = jnp.concatenate(names, axis=1)
     mass = names.shape[1]
     ids = iota((LANES, mass), 0)
-    tall = iota((32, mass), 0)
+    tall = iota((16, mass), 0)
     for j in range(5):
         owner = names[j + 1 : j + 2] if j else names[0:1]
         row = names[j + 5 : j + 6] if j else names[1:2]
         y, z, c = owner // 32, (owner // 2) % 16, owner % 2
-        owners[j] = jnp.where(ids == z * 8 + y * 2 + c, 1.0, 0.0).astype(bf16)
+        at = z * 8 + y * 2 + c
         if j:
-            rows[32 * j - 24 : 32 * j + 8, :] = jnp.where(tall == row, 1.0, 0.0)
+            for side in range(2):
+                hit = ids == jnp.where(row // 16 == side, at, -1)
+                owners[2 * j - 1 + side] = jnp.where(hit, 1.0, 0.0).astype(bf16)
+            rows[16 * j - 8 : 16 * j + 8, :] = jnp.where(tall == row % 16, 1.0, 0.0)
         else:
+            owners[0] = jnp.where(ids == at, 1.0, 0.0).astype(bf16)
             rows[0:8, :] = jnp.where(tall[:8] == row, 1.0, 0.0)
 
 
@@ -171,48 +175,51 @@
     got = dot(table([0]), owners[0])
     mask = rows[0:8, :]
     total = [got[8 * w : 8 * w + 8] * mask for w in range(9)]
-    listed = table([1, 2, 3, 4])
+    listed = jnp.concatenate([table([1, 2]), table([3, 4])], axis=1)
     for j in range(1, 5):
-        got = dot(listed, owners[j])
-        masks = [rows[32 * j - 24 + 8 * o : 32 * j - 16 + 8 * o, :] for o in range(4)]
+        got = dot(listed, jnp.concatenate([owners[2 * j - 1], owners[2 * j]], axis=0))
+        masks = [rows[16 * j - 8 + 8 * o : 16 * j + 8 * o, :] for o in range(2)]
         for w in range(9):
-            for o in range(4):
-                at = 8 * (4 * w + o)
+            for o in range(2):
+                at = 8 * (2 * w + o)
                 total[w] = total[w] + got[at : at + 8] * masks[o]
     total = [jnp.sum(v, axis=0, keepdims=True) for v in total]
-    logits = total[8] * (1.0 / send.shape[0])
+    first = lax.axis_index("y") + lax.axis_index("c") + lax.axis_index("x") == 0
+    logits = jnp.where(first, total[8], 0.0)
     for w in range(4):
         logits = logits + total[w] * total[w + 4]
     sums[...] = jnp.concatenate(total + [jnp.zeros((7, logits.shape[1]), f32)], axis=0)
     logits = jnp.concatenate([logits[:, LANES * b : LANES * (b + 1)] for b in range(8)], axis=0)
+    logits = logits.astype(bf16)
     for p in range(send.shape[0]):
         send[p] = logits
 
 
 def back_kernel(came, labels, sums, owners, rows, send):
-    logits = came[0]
+    logits = came[0].astype(f32)
     for p in range(1, came.shape[0]):
-        logits = logits + came[p]
+        logits = logits + came[p].astype(f32)
     grad = loss_scale * (1.0 / (1.0 + jnp.exp(-logits)) - labels[...])
     grad = jnp.concatenate([grad[b : b + 1] for b in range(8)], axis=1)
     back = [grad * sums[w : w + 1, :] for w in range(8)] + [grad]
 
-    def scatter(j, masks):
+    def scatter(owner, masks):
         tall = jnp.concatenate([mask * value for value in back for mask in masks], axis=0)
-        return dot(tall.astype(bf16), owners[j], 1, 1)
-
-    own = scatter(0, [rows[0:8, :]])
+        return dot(tall.astype(bf16), owner, 1, 1)
+
+    own = scatter(owners[0], [rows[0:8, :]])
     listed = None
     for j in range(1, 5):
-        part = scatter(j, [rows[32 * j - 24 + 8 * o : 32 * j - 16 + 8 * o, :] for o in range(4)])
+        owner = jnp.concatenate([owners[2 * j - 1], owners[2 * j]], axis=0)
+        part = scatter(owner, [rows[16 * j - 8 + 8 * o : 16 * j + 8 * o, :] for o in range(2)])
         listed = part if listed is None else listed + part
     empty = jnp.zeros((8, LANES), f32)
     blocks = [[empty] * TILES for _ in range(16)]
     for w in range(9):
         for o in range(5):
             g, t = unit(w, o)
-            at = 8 * (4 * w + o - 1)
-            blocks[g][t] = listed[at : at + 8] if o else own[8 * w : 8 * w + 8]
+            at, side = 8 * (2 * w + (o - 1) % 2), LANES * ((o - 1) // 2)
+            blocks[g][t] = listed[at : at + 8, side : side + LANES] if o else own[8 * w : 8 * w + 8]
     blocks = exchange(blocks)
     for z in range(send.shape[0]):
         send[z] = jnp.concatenate(blocks[z], axis=0).astype(bf16)
@@ -326,12 +333,12 @@
     table = swap(send, "z")
     owners, rows, targets = call(
         pick_kernel,
-        [shape((5, LANES, mass), bf16), shape((136, mass), f32), shape((8, LANES), f32)],
+        [shape((9, LANES, mass), bf16), shape((72, mass), f32), shape((8, LANES), f32)],
         10_000_000, 3_000_000,
         came,
     )
     send, sums = call(
-        fetch_kernel, [shape((plane, 8, LANES), f32), shape((16, mass), f32)], 400_000_000, 3_000_000,
+        fetch_kernel, [shape((plane, 8, LANES), bf16), shape((16, mass), f32)], 400_000_000, 3_000_000,
         table, owners, rows,
     )
     came = swap(send, BLOCK)

time: 92.6 us -> 92.1 us (level)
  no operation moved by 1% of the time
where the time goes in v4:
time: 92.1 us; the launch traced here: 91.7 us
  blocking collectives  58.4 us (63%)
  starting transfers between devices  13 us (14%)
  waiting for transfers between devices  11 us (12%)
  Pallas kernels  8.53 us (9%)
    all_to_all x4, blocking collectives, swap(): return lax.all_to_all(value, axes, split_axis=0, concat_axis=0, tiled=True)  58.4 us
    all_to_all x1, starting transfers between devices, swap(): return lax.all_to_all(value, axes, split_axis=0, concat_axis=0, tiled=True)  13 us
    all_to_all x1, waiting for transfers between devices, swap(): return lax.all_to_all(value, axes, split_axis=0, concat_axis=0, tiled=True)  11 us
    pallas_call x6, Pallas kernels, call(): pl.pallas_call(kernel, out_shape=outs, in_specs=[spec] * len(args), out_s...  5.32 us
    pallas_call x1, Pallas kernels, call(): pl.pallas_call(kernel, out_shape=outs, grid=(1,), in_specs=[pl.BlockSpec(...  3.21 us
  transfers between devices with their start and end apart: 1, of which 1 were waited for; matrix products, arithmetic and copies ran while one was open for 0% of the time, Pallas kernels for 1%

profile of v4, /device:TPU:1, one launch (start us, length us, event | category | flops | bytes accessed | tf_op | source)
XLA Modules:
  0.0 91.7 jit_solution(10692757416384983498)
XLA Ops:
  0.6 3.2 %shard_map.167 = bf16[32,8,128]{2,1,0:T(8,128)(2,1)} custom-call(bf16[8,4096]{1,0:T(8,128)(2,1)} %table_u.1, bf16[1,8]{1,0:T(2,128)(2,1)} %bitcast.20, bf16[32,256]{1,0:T(8,128)(2,1)} %table_i.1, s32[1,128]{1,0:T(1,128)} %bitcast.21, s32[1,128]{1,0:T(1,128)} %bitcast.22, s32[4,128]{1,0:T(4,128)} %bitcast.18, s32[4,128]{1,0:T(4,128)} %bitcast.19, ...), custom_call_target="tpu_custom_call" | custom-call | flops 20000000 | bytes 2500000 | tf_op jit(solution)/shard_map/pallas_call | solution.py:275
  3.8 17.8 %all_to_all.25.came = bf16[32,8,128]{2,1,0:T(8,128)(2,1)S(1)} all-to-all(bf16[32,8,128]{2,1,0:T(8,128)(2,1)} %shard_map.167), channel_id=1, replica_groups=mesh['y'=4,'z'=16,'c'=2,'x'=4] {'y','c','x'}, dimensions={0} | all-to-all | bytes 131072 | tf_op jit(solution)/shard_map/all_to_all | solution.py:295
  21.6 0.8 shard_map.168
  22.4 13.0 %all-to-all-start.1 = ((bf16[16,24,128]{2,1,0:T(8,128)(2,1)}), bf16[16,24,128]{2,1,0:T(8,128)(2,1)S(1)}, u32[]{:S(2)}, u32[]{:S(2)}) async-start(bf16[16,24,128]{2,1,0:T(8,128)(2,1)} %shard_map.168), calls=%async_computation.1 | async-start | bytes 196608 | tf_op jit(solution)/shard_map/all_to_all | solution.py:295
  35.4 0.9 shard_map.169
  36.3 11.0 %all-to-all-done.1.came = bf16[16,24,128]{2,1,0:T(8,128)(2,1)S(1)} async-done(((bf16[16,24,128]{2,1,0:T(8,128)(2,1)}), bf16[16,24,128]{2,1,0:T(8,128)(2,1)S(1)}, u32[]{:S(2)}, u32[]{:S(2)}) %all-to-all-start.1) | async-done | bytes 98336 | tf_op jit(solution)/shard_map/all_to_all | solution.py:295
  47.3 0.9 %shard_map.170 = (bf16[32,8,128]{2,1,0:T(8,128)(2,1)S(1)}, f32[16,1024]{1,0:T(8,128)S(1)}) custom-call(bf16[16,24,128]{2,1,0:T(8,128)(2,1)S(1)} %all-to-all-done.1.came, bf16[9,128,1024]{2,1,0:T(8,128)(2,1)S(1)} %get-tuple-element.7.owners, f32[72,1024]{1,0:T(8,128)S(1)} %get-tuple-element.8.rows), custom_call_target="tpu_custom_call" | custom-call | flops 400000000 | bytes 3000000 | tf_op jit(solution)/shard_map/pallas_call | solution.py:284
  48.3 0.0 copy-start
  48.3 0.0 copy-start.1
  48.3 0.0 copy-start.2
  48.3 0.0 copy-start.3
  48.3 0.0 copy-start.4
  48.3 0.0 copy-start.5
  48.3 0.0 copy-start.6
  48.4 0.0 copy-start.7
  48.4 13.0 %all_to_all.26.came = bf16[32,8,128]{2,1,0:T(8,128)(2,1)S(1)} all-to-all(bf16[32,8,128]{2,1,0:T(8,128)(2,1)S(1)} %get-tuple-element.9), channel_id=1, replica_groups=mesh['y'=4,'z'=16,'c'=2,'x'=4] {'y','c','x'}, dimensions={0} | all-to-all | bytes 131072 | tf_op jit(solution)/shard_map/all_to_all | solution.py:295
  61.3 1.1 %shard_map.171 = bf16[16,24,128]{2,1,0:T(8,128)(2,1)S(1)} custom-call(bf16[32,8,128]{2,1,0:T(8,128)(2,1)S(1)} %all_to_all.26.came, f32[8,128]{1,0:T(8,128)S(1)} %get-tuple-element.10.labels, f32[16,1024]{1,0:T(8,128)S(1)} %get-tuple-element.11.sums, bf16[9,128,1024]{2,1,0:T(8,128)(2,1)S(1)} %get-tuple-element.7.owners, f32[72,1024]{1,0:T(8,128)S(1)} %get-tuple-element.8.rows), custom_call_target="tpu_custom_call" | custom-call | flops 400000000 | bytes 3000000 | tf_op jit(solution)/shard_map/pallas_call | solution.py:284
  62.5 14.9 %all_to_all.27.came = bf16[16,24,128]{2,1,0:T(8,128)(2,1)S(1)} all-to-all(bf16[16,24,128]{2,1,0:T(8,128)(2,1)S(1)} %shard_map.171), channel_id=1, replica_groups=mesh['y'=4,'z'=16,'c'=2,'x'=4] {'z'}, dimensions={0} | all-to-all | bytes 196608 | tf_op jit(solution)/shard_map/all_to_all | solution.py:295
  77.3 0.2 shard_map.172
  77.5 12.8 %all_to_all.28.refs_0_ = bf16[32,8,128]{2,1,0:T(8,128)(2,1)S(1)} all-to-all(bf16[32,8,128]{2,1,0:T(8,128)(2,1)S(1)} %shard_map.172), channel_id=1, replica_groups=mesh['y'=4,'z'=16,'c'=2,'x'=4] {'y','c','x'}, dimensions={0} | all-to-all | bytes 131072 | tf_op jit(solution)/shard_map/all_to_all | solution.py:295
  90.3 0.0 copy-done
  90.3 0.0 copy-done.1
  90.3 0.0 copy-done.2
  90.4 1.4 %shard_map.173 = (f32[8,4096]{1,0:T(8,128)}, f32[32,256]{1,0:T(8,128)}) custom-call(bf16[32,8,128]{2,1,0:T(8,128)(2,1)S(1)} %all_to_all.28.refs_0_, bf16[4096,128]{1,0:T(8,128)(2,1)S(1)} %copy-done, bf16[256,128]{1,0:T(8,128)(2,1)S(1)} %copy-done.2, bf16[128,4096]{1,0:T(8,128)(2,1)S(1)} %copy-done.1, bf16[128,256]{1,0:T(8,128)(2,1)S(1)} %copy-done.3, ...), custom_call_target="tpu_custom_call" | custom-call | flops 20000000 | bytes 2500000 | tf_op jit(solution)/shard_map/pallas_call | solution.py:284
  (5 shorter events, 0.0 us)
Async XLA Ops:
  22.4 24.9 %all-to-all-start.1 = ((bf16[16,24,128]{2,1,0:T(8,128)(2,1)}), bf16[16,24,128]{2,1,0:T(8,128)(2,1)S(1)}, u32[]{:S(2)}, u32[]{:S(2)}) async-start(bf16[16,24,128]{2,1,0:T(8,128)(2,1)} %shard_map.168), calls=%async_computation.1 | async-start | bytes 196608 | tf_op jit(solution)/shard_map/all_to_all | solution.py:295
  48.3 42.1 %copy-start = (bf16[4096,128]{1,0:T(8,128)(2,1)S(1)}, bf16[4096,128]{1,0:T(8,128)(2,1)}, u32[]{:S(2)}) copy-start(bf16[4096,128]{1,0:T(8,128)(2,1)} %refs_1_.1) | copy-start | bytes 3145732
  48.3 42.1 %copy-start.1 = (bf16[128,4096]{1,0:T(8,128)(2,1)S(1)}, bf16[128,4096]{1,0:T(8,128)(2,1)}, u32[]{:S(2)}) copy-start(bf16[128,4096]{1,0:T(8,128)(2,1)} %refs_3_.1) | copy-start | bytes 3145732
  48.3 42.0 %copy-start.2 = (bf16[256,128]{1,0:T(8,128)(2,1)S(1)}, bf16[256,128]{1,0:T(8,128)(2,1)}, u32[]{:S(2)}) copy-start(bf16[256,128]{1,0:T(8,128)(2,1)} %refs_2_.1) | copy-start | bytes 196612
  48.3 42.0 %copy-start.3 = (bf16[128,256]{1,0:T(8,128)(2,1)S(1)}, bf16[128,256]{1,0:T(8,128)(2,1)}, u32[]{:S(2)}) copy-start(bf16[128,256]{1,0:T(8,128)(2,1)} %refs_4_.1) | copy-start | bytes 196612
  48.3 42.0 %copy-start.4 = (f32[4096]{0:T(1024)S(1)}, f32[4096]{0:T(1024)}, u32[]{:S(2)}) copy-start(f32[4096]{0:T(1024)} %param.28) | copy-start | bytes 49156
  48.3 42.0 %copy-start.5 = (f32[4096]{0:T(1024)S(1)}, f32[4096]{0:T(1024)}, u32[]{:S(2)}) copy-start(f32[4096]{0:T(1024)} %param.30) | copy-start | bytes 49156
  48.3 42.0 %copy-start.6 = (f32[256]{0:T(256)S(1)}, f32[256]{0:T(256)}, u32[]{:S(2)}) copy-start(f32[256]{0:T(256)} %param.29) | copy-start | bytes 3076
  48.4 42.0 %copy-start.7 = (f32[256]{0:T(256)S(1)}, f32[256]{0:T(256)}, u32[]{:S(2)}) copy-start(f32[256]{0:T(256)} %param.31) | copy-start | bytes 3076
